TPU v7x, 128 devices: a whole 4x4x4 slice. The times are simulated.
128 devices in a mesh: brow: 8 (over x_hi, z), bcol: 16 (over y, x_lo, core).
Axes of the slice: x: 4 (x_hi: 2, x_lo: 2; x = x_hi * 2 + x_lo), y: 4, z: 4, core: 2. Of those that a mesh axis runs over, the one named last changes fastest.
Arguments:
- x_start: float32 [131072, 32], P(('brow', 'bcol')), may hold values from -6 to 6
- bin_mask: int32 [131072], P(('brow', 'bcol')), may hold values 0 or 1
- band: bfloat16 [512, 16, 256, 256], P('brow', 'bcol'), may hold values from -0.0625 to 0.0625
- off_tiles: bfloat16 [8, 16, 64, 256, 256], P('brow', 'bcol'), may hold values from -0.0625 to 0.0625
- off_rows: int32 [8, 16, 64], P('brow', 'bcol'), may hold values from 0 to 63
- off_cols: int32 [8, 16, 64], P('brow', 'bcol'), may hold values from 0 to 31
- off_count: int32 [8, 16], P('brow', 'bcol'), may hold values from 32 to 64, as said below
Outputs:
- eigen_block: float32 [131072, 32], P(('brow', 'bcol'))
- ritz_matrix: float32 [32, 32], replicated
Inputs may be any that keep to these rules, and one draw needn't show every extreme that they name: `off_count`: slots at and beyond a device's count hold no tile; some device uses all 64 slots; coordinates on a device may repeat.
All inputs are finite; a program needn't handle non-finite values. No bound on the sum of `bin_mask` on one device may be relied on, other than what follows from the above.
Results may differ from a plain program's by a relative error of at most 0.0026.
Values may be sent and summed in bfloat16 or wider, within the bound.
No kernel may reach another device: no remote copies, remote signals or barrier semaphores. Data moves between devices by JAX's collectives and lax.ppermute only.
A program may use at most 128 MiB of HBM per device.

v0:
```python
import jax
import jax.numpy as jnp
from jax import lax
from jax.sharding import PartitionSpec as P

STEPS = 3


PRECISE = lax.Precision.HIGHEST
EPSILON = 1e-06


def shifted(value, axis, by):
    length = lax.axis_size(axis)
    pairs = [(i, i + by) for i in range(length) if 0 <= i + by < length]
    return lax.ppermute(value, axis, pairs)


def gram_of(left, right):
    return jnp.dot(left.T, right, precision=PRECISE, preferred_element_type=jnp.float32)


def symmetric(matrix):
    return 0.5 * (matrix + matrix.T)


def right_solve(values, factor):
    return lax.linalg.triangular_solve(
        factor, values, left_side=False, lower=True, transpose_a=True
    )


def left_solve(factor, values, transposed):
    return lax.linalg.triangular_solve(
        factor, values, left_side=True, lower=True, transpose_a=transposed
    )


def projected(factor, matrix):
    return symmetric(right_solve(left_solve(factor, matrix, False), factor))


def rayleigh_ritz(basis_gram, image_gram, block_width):
    factor = jnp.linalg.cholesky(basis_gram)
    reduced = projected(factor, image_gram)
    basis_order = reduced.shape[0]
    scaling = jnp.sqrt(jnp.sum(reduced * reduced))
    filtered = (reduced + scaling * jnp.eye(basis_order, dtype=jnp.float32)) / (2.0 * scaling)
    filtered = jnp.dot(filtered, filtered, precision=PRECISE)
    filtered = jnp.dot(filtered, filtered, precision=PRECISE)
    leading = filtered[:, :block_width]
    small_factor = jnp.linalg.cholesky(gram_of(leading, leading))
    orthonormal = right_solve(leading, small_factor)
    return left_solve(factor, orthonormal, True)


def body(x_start, bin_mask, band, off_tiles, off_rows, off_cols, off_count):
    tile_size = band.shape[2]
    block_width = x_start.shape[1]
    row_tiles = band.shape[0]
    band_local = band.shape[1]
    bands = band_local * lax.axis_size("bcol")
    col_index = lax.axis_index("bcol")
    mask_float = bin_mask.astype(jnp.float32)[:, None]
    tiles_local = off_tiles[0, 0]
    rows_local = off_rows[0, 0]
    cols_local = off_cols[0, 0]
    live_slots = (jnp.arange(tiles_local.shape[0], dtype=jnp.int32) < off_count[0, 0]).astype(
        jnp.float32
    )[:, None, None]

    def operator_core(row_b, slab_b):
        col_b = lax.all_gather(slab_b, "brow", axis=0, tiled=True)
        row_t = row_b.reshape(row_tiles, tile_size, block_width)
        col_t = col_b.reshape(-1, tile_size, block_width)
        rim_rows = shifted(row_b[: (bands - 1) * tile_size], "brow", -1)
        extended = jnp.concatenate(
            [row_t, rim_rows.reshape(bands - 1, tile_size, block_width)], axis=0
        )
        spread = jnp.zeros((row_tiles + bands - 1, tile_size, block_width), jnp.float32)
        offset = 0
        shift_by = col_index * band_local + offset
        blocks = band[:, offset]
        returned = jnp.einsum("nba,nbk->nak", blocks, row_t, preferred_element_type=jnp.float32)
        spread = lax.dynamic_update_slice_in_dim(spread, returned, shift_by, 0)
        spilled = shifted(spread[row_tiles:], "brow", 1)
        rest_rows = spread[:row_tiles]
        rest_rows = rest_rows.at[: bands - 1].add(spilled)
        far_forward = (
            jnp.einsum(
                "sab,sbk->sak", tiles_local, col_t[cols_local], preferred_element_type=jnp.float32
            )
            * live_slots
        )
        far_back = (
            jnp.einsum(
                "sba,sbk->sak", tiles_local, row_t[rows_local], preferred_element_type=jnp.float32
            )
            * live_slots
        )
        rest_rows = rest_rows.at[rows_local].add(far_forward)
        crossed = jnp.zeros(col_t.shape, jnp.float32).at[cols_local].add(far_back)
        offset = 0
        shift_by = col_index * band_local + offset
        blocks = band[:, offset]
        nearby = lax.dynamic_slice_in_dim(extended, shift_by + 0, row_tiles, 0)
        total = jnp.einsum("nab,nbk->nak", blocks, nearby, preferred_element_type=jnp.float32)
        own_rows = total + rest_rows
        part_rows = lax.psum_scatter(
            own_rows.reshape(-1, block_width), "bcol", scatter_dimension=0, tiled=True
        )
        part_cols = lax.psum_scatter(
            crossed.reshape(-1, block_width), "brow", scatter_dimension=0, tiled=True
        )
        return (part_rows + part_cols) * mask_float

    started = x_start * mask_float

    def apply_operator(vectors):
        slab_b = (vectors * mask_float).astype(jnp.bfloat16)
        row_b = lax.all_gather(slab_b, "bcol", axis=0, tiled=True)
        return operator_core(row_b, slab_b)

    def global_sum(parts):
        return lax.psum(parts, ("brow", "bcol"))

    first_image = apply_operator(started)
    factor = jnp.linalg.cholesky(global_sum(gram_of(started, started)))
    vectors = right_solve(started, factor)
    images_now = right_solve(first_image, factor)
    previous = ()
    for iteration in range(STEPS):
        ritz_now = symmetric(global_sum(gram_of(vectors, images_now)))
        residual = images_now - jnp.dot(vectors, ritz_now, precision=PRECISE)
        residual_image = apply_operator(residual)
        tail_cols = jnp.concatenate([residual] + list(previous[:1]), axis=1)
        tail_images = jnp.concatenate([residual_image] + list(previous[1:]), axis=1)
        col_norms = global_sum(jnp.sum(tail_cols * tail_cols, axis=0))
        scaling = lax.rsqrt(col_norms + EPSILON)
        basis_cols = jnp.concatenate([vectors, tail_cols * scaling[None, :]], axis=1)
        image_cols = jnp.concatenate([images_now, tail_images * scaling[None, :]], axis=1)
        basis_gram, image_gram = global_sum(
            (gram_of(basis_cols, basis_cols), gram_of(basis_cols, image_cols))
        )
        image_gram = symmetric(image_gram)
        weights = rayleigh_ritz(basis_gram, image_gram, block_width)
        vectors = jnp.dot(basis_cols, weights, precision=PRECISE)
        images_now = jnp.dot(image_cols, weights, precision=PRECISE)
        tail_weights = weights[block_width:]
        previous = (
            jnp.dot(basis_cols[:, block_width:], tail_weights, precision=PRECISE),
            jnp.dot(image_cols[:, block_width:], tail_weights, precision=PRECISE),
        )
    ritz_final = symmetric(global_sum(gram_of(vectors, images_now)))
    return (vectors, ritz_final)


def solution(mesh):
    return jax.shard_map(
        body,
        mesh=mesh,
        in_specs=(
            P(("brow", "bcol"), None),
            P(("brow", "bcol")),
            P("brow", "bcol", None, None),
            P("brow", "bcol", None, None, None),
            P("brow", "bcol", None),
            P("brow", "bcol", None),
            P("brow", "bcol"),
        ),
        out_specs=(P(("brow", "bcol"), None), P()),
        check_vma=False,
    )
```

profile of v0, /device:TPU:0, one launch (start us, length us, event | category | flops | bytes accessed | tf_op | source)
XLA Modules:
  0.0 1545.6 jit_solution(9406066421393951599)
XLA Ops:
  9.5 37.2 %all_gather.25 = bf16[8192,32]{0,1:T(8,128)(2,1)S(1)} all-gather(bf16[1024,32]{0,1:T(8,128)(2,1)} %multiply_convert_fusion.3), channel_id=1, replica_groups=mesh['brow'=8,'bcol'=16] {'brow'}, dimensions={0}, use_global_device_ids=true | all-gather | bytes 589824 | tf_op jit(solution)/shard_map/all_gather | solution.py:73
  57.2 7.0 scatter_fusion.1
  87.8 7.0 scatter_fusion
  97.6 68.9 %psum.98 = f32[32,32]{0,1:T(8,128)S(1)} all-reduce(f32[32,32]{0,1:T(8,128)S(1)} %fusion.93), channel_id=1, replica_groups=mesh['brow'=8,'bcol'=16] {'brow','bcol'}, use_global_device_ids=true, to_apply=%region_0.0 | all-reduce | flops 1024 | bytes 8192 | tf_op jit(solution)/shard_map/psum | solution.py:125
  173.6 34.9 %reduce-scatter.9.cloned.1.call-done = f32[1024,32]{0,1:T(8,128)} async-done(((f32[16384,32]{0,1:T(8,128)}), f32[1024,32]{0,1:T(8,128)}) %reduce-scatter.9.cloned.1.call-update) | async-done | bytes 131088 | tf_op jit(solution)/shard_map/reduce_scatter | solution.py:109
  210.1 64.9 %psum.99 = f32[32,32]{1,0:T(8,128)S(1)} all-reduce(f32[32,32]{1,0:T(8,128)S(1)} %fusion.228), channel_id=1, replica_groups=mesh['brow'=8,'bcol'=16] {'brow','bcol'}, use_global_device_ids=true, to_apply=%region_7.10 | all-reduce | flops 1024 | bytes 8192 | tf_op jit(solution)/shard_map/psum | solution.py:125
  275.5 62.3 %psum.100 = f32[32]{0:T(128)S(1)} all-reduce(f32[32]{0:T(128)S(1)} %get-tuple-element.69), channel_id=1, replica_groups=mesh['brow'=8,'bcol'=16] {'brow','bcol'}, use_global_device_ids=true, to_apply=%region_9.12 | all-reduce | flops 32 | bytes 256 | tf_op jit(solution)/shard_map/psum | solution.py:125
  338.5 29.9 %all-gather.7.cloned.1.call-done = bf16[16384,32]{0,1:T(8,128)(2,1)} async-done(((bf16[1024,32]{0,1:T(8,128)(2,1)}), bf16[16384,32]{0,1:T(8,128)(2,1)}) %all-gather.7.cloned.1.call-update) | async-done | bytes 1048592 | tf_op jit(solution)/shard_map/all_gather | solution.py:121
  376.9 7.0 scatter_fusion.3
  385.1 35.6 %all_gather.27 = bf16[8192,32]{0,1:T(8,128)(2,1)S(1)} all-gather(bf16[1024,32]{0,1:T(8,128)(2,1)S(1)} %copy-done.14), channel_id=1, replica_groups=mesh['brow'=8,'bcol'=16] {'brow'}, dimensions={0}, use_global_device_ids=true | all-gather | bytes 589824 | tf_op jit(solution)/shard_map/all_gather | solution.py:73
  442.5 7.0 scatter_fusion.2
  458.1 65.9 %reduce-scatter.13.cloned.1.call-done = f32[1024,32]{0,1:T(8,128)} async-done(((f32[16384,32]{0,1:T(8,128)}), f32[1024,32]{0,1:T(8,128)}) %reduce-scatter.13.cloned.1.call-update) | async-done | bytes 131088 | tf_op jit(solution)/shard_map/reduce_scatter | solution.py:109
  525.4 76.6 %all-reduce.2 = (f32[64,64]{0,1:T(8,128)S(1)}, f32[64,64]{0,1:T(8,128)S(1)}) all-reduce(f32[64,64]{0,1:T(8,128)S(1)} %fusion.87, f32[64,64]{0,1:T(8,128)S(1)} %fusion.89), channel_id=1, replica_groups=mesh['brow'=8,'bcol'=16] {'brow','bcol'}, use_global_device_ids=true, to_apply=%region_17.0 | all-reduce | flops 8192 | bytes 65536 | tf_op jit(solution)/shard_map/psum | solution.py:125
  624.7 62.2 %psum.103 = f32[32,32]{0,1:T(8,128)S(1)} all-reduce(f32[32,32]{0,1:T(8,128)S(1)} %fusion.230), channel_id=1, replica_groups=mesh['brow'=8,'bcol'=16] {'brow','bcol'}, use_global_device_ids=true, to_apply=%region_19.0 | all-reduce | flops 1024 | bytes 8192 | tf_op jit(solution)/shard_map/psum | solution.py:125
  688.1 29.8 %all-gather.9.cloned.1.call-done = bf16[16384,32]{0,1:T(8,128)(2,1)} async-done(((bf16[1024,32]{0,1:T(8,128)(2,1)}), bf16[16384,32]{0,1:T(8,128)(2,1)}) %all-gather.9.cloned.1.call-update) | async-done | bytes 1048592 | tf_op jit(solution)/shard_map/all_gather | solution.py:121
  726.4 7.0 scatter_fusion.5
  734.6 35.5 %all_gather.29 = bf16[8192,32]{0,1:T(8,128)(2,1)S(1)} all-gather(bf16[1024,32]{0,1:T(8,128)(2,1)S(1)} %copy-done.13), channel_id=1, replica_groups=mesh['brow'=8,'bcol'=16] {'brow'}, dimensions={0}, use_global_device_ids=true | all-gather | bytes 589824 | tf_op jit(solution)/shard_map/all_gather | solution.py:73
  792.0 7.0 scatter_fusion.4
  801.8 68.7 %psum.104 = f32[64]{0:T(128)S(1)} all-reduce(f32[64]{0:T(128)S(1)} %multiply_reduce_fusion.1), channel_id=1, replica_groups=mesh['brow'=8,'bcol'=16] {'brow','bcol'}, use_global_device_ids=true, to_apply=%region_21.0 | all-reduce | flops 64 | bytes 512 | tf_op jit(solution)/shard_map/psum | solution.py:125
  878.4 137.8 %all-reduce.8.cloned.1.call-done = (f32[96,96]{1,0:T(8,128)}, f32[96,96]{0,1:T(8,128)}) async-done(((f32[96,96]{1,0:T(8,128)}, f32[96,96]{0,1:T(8,128)}), (f32[96,96]{1,0:T(8,128)}, f32[96,96]{0,1:T(8,128)})) %all-reduce.8.cloned.1.call-update) | async-done | bytes 73744 | tf_op jit(solution)/shard_map/psum | solution.py:125
  1018.8 8.8 cholesky.175
  1028.9 7.4 custom-call.44
  1047.8 64.5 %psum.107 = f32[32,32]{0,1:T(8,128)S(1)} all-reduce(f32[32,32]{0,1:T(8,128)S(1)} %fusion.232), channel_id=1, replica_groups=mesh['brow'=8,'bcol'=16] {'brow','bcol'}, use_global_device_ids=true, to_apply=%region_31.39 | all-reduce | flops 1024 | bytes 8192 | tf_op jit(solution)/shard_map/psum | solution.py:125
  1113.4 29.0 %all-gather.11.cloned.1.call-done = bf16[16384,32]{0,1:T(8,128)(2,1)} async-done(((bf16[1024,32]{0,1:T(8,128)(2,1)}), bf16[16384,32]{0,1:T(8,128)(2,1)}) %all-gather.11.cloned.1.call-update) | async-done | bytes 1048592 | tf_op jit(solution)/shard_map/all_gather | solution.py:121
  1150.9 7.0 scatter_fusion.7
  1159.1 35.5 %all_gather.31 = bf16[8192,32]{0,1:T(8,128)(2,1)S(1)} all-gather(bf16[1024,32]{0,1:T(8,128)(2,1)S(1)} %copy-done.12), channel_id=1, replica_groups=mesh['brow'=8,'bcol'=16] {'brow'}, dimensions={0}, use_global_device_ids=true | all-gather | bytes 589824 | tf_op jit(solution)/shard_map/all_gather | solution.py:73
  1216.6 7.0 scatter_fusion.6
  1226.3 68.8 %psum.108 = f32[64]{0:T(128)S(1)} all-reduce(f32[64]{0:T(128)S(1)} %multiply_reduce_fusion), channel_id=1, replica_groups=mesh['brow'=8,'bcol'=16] {'brow','bcol'}, use_global_device_ids=true, to_apply=%region_33.41 | all-reduce | flops 64 | bytes 512 | tf_op jit(solution)/shard_map/psum | solution.py:125
  1301.6 139.1 %all-reduce.6.cloned.1.call-done = (f32[96,96]{0,1:T(8,128)}, f32[96,96]{0,1:T(8,128)}) async-done(((f32[96,96]{0,1:T(8,128)}, f32[96,96]{0,1:T(8,128)}), (f32[96,96]{0,1:T(8,128)}, f32[96,96]{0,1:T(8,128)})) %all-reduce.6.cloned.1.call-update) | async-done | bytes 73744 | tf_op jit(solution)/shard_map/psum | solution.py:125
  1443.3 8.8 cholesky.197
  1453.4 7.4 custom-call.48
  1473.7 64.5 %psum.111 = f32[32,32]{0,1:T(8,128)S(1)} all-reduce(f32[32,32]{0,1:T(8,128)S(1)} %fusion.234), channel_id=1, replica_groups=mesh['brow'=8,'bcol'=16] {'brow','bcol'}, use_global_device_ids=true, to_apply=%region_41.49 | all-reduce | flops 1024 | bytes 8192 | tf_op jit(solution)/shard_map/psum | solution.py:125
  (331 shorter events, 227.0 us)
Async XLA Ops:
  7.2 41.7 %all-gather.5.cloned.1.call-start = ((), (), s32[]{:S(2)}) async-start(), calls=%async_computation.8 | async-start | bytes 1114112 | tf_op jit(solution)/shard_map/all_gather | solution.py:121
  9.5 164.1 %reduce-scatter.11.cloned.1.call-start = ((), (), s32[]{:S(2)}) async-start(), calls=%async_computation.10 | async-start | bytes 1179648 | tf_op jit(solution)/shard_map/reduce_scatter | solution.py:112
  65.3 143.3 %reduce-scatter.9.cloned.1.call-start = ((), (), s32[]{:S(2)}) async-start(), calls=%async_computation.9 | async-start | bytes 2228224 | tf_op jit(solution)/shard_map/reduce_scatter | solution.py:109
  71.8 13.4 collective-permute-start.1
  76.0 9.1 collective-permute-start
  96.4 272.0 %all-gather.7.cloned.1.call-start = ((), (), s32[]{:S(2)}) async-start(), calls=%async_computation.11 | async-start | bytes 1114112 | tf_op jit(solution)/shard_map/all_gather | solution.py:121
  338.5 119.6 %reduce-scatter.15.cloned.1.call-start = ((), (), s32[]{:S(2)}) async-start(), calls=%async_computation.13 | async-start | bytes 1179648 | tf_op jit(solution)/shard_map/reduce_scatter | solution.py:112
  385.0 139.0 %reduce-scatter.13.cloned.1.call-start = ((), (), s32[]{:S(2)}) async-start(), calls=%async_computation.12 | async-start | bytes 2228224 | tf_op jit(solution)/shard_map/reduce_scatter | solution.py:109
  427.2 12.6 collective-permute-start.3
  431.5 8.4 collective-permute-start.2
  451.1 266.8 %all-gather.9.cloned.1.call-start = ((), (), s32[]{:S(2)}) async-start(), calls=%async_computation.14 | async-start | bytes 1114112 | tf_op jit(solution)/shard_map/all_gather | solution.py:121
  525.0 192.9 %copy-start.8 = (f32[1024,32]{0,1:T(8,128)}, f32[1024,32]{0,1:T(8,128)S(1)}, u32[]{:S(2)}) copy-start(f32[1024,32]{0,1:T(8,128)S(1)} %multiply_multiply_fusion) | copy-start | bytes 393220
  623.9 94.0 %copy-start.18 = (f32[64,32]{0,1:T(8,128)}, f32[64,32]{0,1:T(8,128)S(1)}, u32[]{:S(2)}) copy-start(f32[64,32]{0,1:T(8,128)S(1)} %fusion.139) | copy-start | bytes 24580
  624.2 93.7 %copy-start.6 = (f32[1024,32]{0,1:T(8,128)}, f32[1024,32]{0,1:T(8,128)S(1)}, u32[]{:S(2)}) copy-start(f32[1024,32]{0,1:T(8,128)S(1)} %fusion.86) | copy-start | bytes 393220
  688.0 113.6 %copy-start.11 = (f32[1024,32]{0,1:T(8,128)}, f32[1024,32]{0,1:T(8,128)S(1)}, u32[]{:S(2)}) copy-start(f32[1024,32]{0,1:T(8,128)S(1)} %get-tuple-element.72) | copy-start | bytes 393220
  688.0 182.8 %reduce-scatter.19.cloned.1.call-start = ((), (), s32[]{:S(2)}) async-start(), calls=%async_computation.16 | async-start | bytes 1179648 | tf_op jit(solution)/shard_map/reduce_scatter | solution.py:112
  734.5 139.2 %reduce-scatter.17.cloned.1.call-start = ((), (), s32[]{:S(2)}) async-start(), calls=%async_computation.15 | async-start | bytes 2228224 | tf_op jit(solution)/shard_map/reduce_scatter | solution.py:109
  776.7 12.7 collective-permute-start.5
  781.0 8.4 collective-permute-start.4
  800.6 76.2 %copy-start.7 = (f32[1024,32]{0,1:T(8,128)S(1)}, f32[1024,32]{0,1:T(8,128)}, u32[]{:S(2)}) copy-start(f32[1024,32]{0,1:T(8,128)} %copy-done.6) | copy-start | bytes 393220
  800.6 215.6 %all-reduce.8.cloned.1.call-start = ((), (), s32[]{:S(2)}) async-start(), calls=%async_computation.21 | async-start | bytes 196608 | tf_op jit(solution)/shard_map/psum | solution.py:125
  875.7 171.1 %copy-start.2 = (f32[1024,64]{0,1:T(8,128)}, f32[1024,64]{0,1:T(8,128)S(1)}, u32[]{:S(2)}) copy-start(f32[1024,64]{0,1:T(8,128)S(1)} %get-tuple-element.68) | copy-start | bytes 786436
  877.9 264.5 %all-gather.11.cloned.1.call-start = ((), (), s32[]{:S(2)}) async-start(), calls=%async_computation.17 | async-start | bytes 1114112 | tf_op jit(solution)/shard_map/all_gather | solution.py:121
  1046.8 95.6 %copy-start.16 = (f32[96,32]{0,1:T(8,128)}, f32[96,32]{0,1:T(8,128)S(1)}, u32[]{:S(2)}) copy-start(f32[96,32]{0,1:T(8,128)S(1)} %fusion.119) | copy-start | bytes 36868
  1047.2 95.3 %copy-start.4 = (f32[1024,32]{0,1:T(8,128)}, f32[1024,32]{0,1:T(8,128)S(1)}, u32[]{:S(2)}) copy-start(f32[1024,32]{0,1:T(8,128)S(1)} %fusion.78) | copy-start | bytes 393220
  1047.5 94.9 %copy-start = (f32[1024,32]{0,1:T(8,128)}, f32[1024,32]{0,1:T(8,128)S(1)}, u32[]{:S(2)}) copy-start(f32[1024,32]{0,1:T(8,128)S(1)} %fusion.82) | copy-start | bytes 393220
  1113.4 182.1 %reduce-scatter.23.cloned.1.call-start = ((), (), s32[]{:S(2)}) async-start(), calls=%async_computation.19 | async-start | bytes 1179648 | tf_op jit(solution)/shard_map/reduce_scatter | solution.py:112
  1159.0 139.3 %reduce-scatter.21.cloned.1.call-start = ((), (), s32[]{:S(2)}) async-start(), calls=%async_computation.18 | async-start | bytes 2228224 | tf_op jit(solution)/shard_map/reduce_scatter | solution.py:109
  1201.2 12.7 collective-permute-start.7
  1205.5 8.4 collective-permute-start.6
  1225.1 75.4 %copy-start.5 = (f32[1024,32]{0,1:T(8,128)S(1)}, f32[1024,32]{0,1:T(8,128)}, u32[]{:S(2)}) copy-start(f32[1024,32]{0,1:T(8,128)} %copy-done.4) | copy-start | bytes 393220
  1225.2 215.6 %all-reduce.6.cloned.1.call-start = ((), (), s32[]{:S(2)}) async-start(), calls=%async_computation.20 | async-start | bytes 196608 | tf_op jit(solution)/shard_map/psum | solution.py:125
  (30 other events, 559.9 us)
Sparse Core Ops, SparseCore 0:
  10.2 35.1 all-gather.4
  65.4 76.7 reduce-scatter.10
  144.8 63.7 reduce-scatter.8
  338.6 29.7 all-gather.6
  385.1 72.9 reduce-scatter.14
  460.3 63.5 reduce-scatter.12
  688.2 29.6 all-gather.8
  734.6 72.9 reduce-scatter.18
  810.1 63.5 reduce-scatter.16
  879.8 136.3 all-reduce.7
  1113.5 28.9 all-gather.10
  1159.2 72.9 reduce-scatter.22
  1234.6 63.6 reduce-scatter.20
  1304.4 136.2 all-reduce.5
where the time goes:
time: 1550 us
  blocking collectives  745 us (48%)
  waiting for transfers between devices  491 us (32%)
  other arithmetic  143 us (9%)
  matrix products  93 us (6%)
  local copies, waits for them, and re-layouts  35.5 us (2%)
  starting transfers between devices  19.9 us (1%)
  between operations  18.4 us (1%)
    psum x9, blocking collectives, global_sum(): return lax.psum(parts, ('brow', 'bcol'))  601 us
    psum x2, waiting for transfers between devices, global_sum(): return lax.psum(parts, ('brow', 'bcol'))  277 us
    all_gather x4, blocking collectives, operator_core(): col_b = lax.all_gather(slab_b, 'brow', axis=0, tiled=True)  144 us
    reduce_scatter x4, waiting for transfers between devices, operator_core(): lax.psum_scatter(own_rows.reshape(-1, block_width), 'bcol', scatter_dimen...  107 us
    all_gather x4, waiting for transfers between devices, apply_operator(): row_b = lax.all_gather(slab_b, 'bcol', axis=0, tiled=True)  88.7 us
  transfers between devices with their start and end apart: 22, of which 14 were waited for; matrix products, arithmetic and copies ran while one was open for 7% of the time, Pallas kernels for 0%

commit v1 on v0

v1 whole, which is shorter than its diff:
```python
import functools

import jax
import jax.numpy as jnp
from jax import lax
from jax.experimental import pallas as pl
from jax.experimental.pallas import tpu as pltpu
from jax.sharding import PartitionSpec as P

STEPS = 3
PRECISE = lax.Precision.HIGHEST
EPSILON = 1e-06
F32 = jnp.float32
BF16 = jnp.bfloat16
GROUP = 8
VMEM_BYTES = 40 * 1024 * 1024


def flip(value, axis, by):
    length = lax.axis_size(axis)
    return lax.ppermute(value, axis, [(i, i ^ by) for i in range(length)])


def flip_both(value, row_by, col_by):
    rows, cols = lax.axis_size("brow"), lax.axis_size("bcol")
    pairs = [
        (r * cols + c, (r ^ row_by) * cols + (c ^ col_by)) for r in range(rows) for c in range(cols)
    ]
    return lax.ppermute(value, ("brow", "bcol"), pairs)


def shifted(value, axis, by):
    length = lax.axis_size(axis)
    pairs = [(i, i + by) for i in range(length) if 0 <= i + by < length]
    return lax.ppermute(value, axis, pairs)


def sum_all(value):
    value = value + flip(value, "bcol", 1)
    value = (value + flip(value, "bcol", 4)) + (flip(value, "bcol", 8) + flip(value, "bcol", 12))
    value = (value + flip(value, "brow", 1)) + (flip(value, "brow", 2) + flip(value, "brow", 3))
    value = (value + flip(value, "bcol", 2)) + (flip(value, "brow", 4) + flip_both(value, 4, 2))
    return value


def whole(shape):
    return pl.BlockSpec(shape, lambda *_: (0,) * len(shape))


def params():
    return pltpu.CompilerParams(vmem_limit_bytes=VMEM_BYTES)


def assemble_kernel(ids, p0, p1, p2, p3, q0, q1, q2, q3, rows_out, rim_out):
    me = ids[1]
    for s in range(16):
        slot = me ^ s
        core, half, quarter = slot & 1, (slot >> 1) & 1, slot >> 2
        for k in range(4):
            for parity, ref in ((0, (p0, p1, p2, p3)[k]), (1, (q0, q1, q2, q3)[k])):

                @pl.when((quarter == k) & (core == parity))
                def _():
                    rows_out[4 * s : 4 * s + 4] = ref[half]
                    if s < 4:
                        rim_out[4 * s : 4 * s + 4] = ref[half]


def assemble(ids, parts):
    return pl.pallas_call(
        assemble_kernel,
        grid_spec=pltpu.PrefetchScalarGridSpec(
            num_scalar_prefetch=1,
            grid=(1,),
            in_specs=[whole((2, 4, 32, 256))] * 8,
            out_specs=[whole((64, 32, 256)), whole((16, 32, 256))],
        ),
        out_shape=[
            jax.ShapeDtypeStruct((64, 32, 256), BF16),
            jax.ShapeDtypeStruct((16, 32, 256), BF16),
        ],
        compiler_params=params(),
        cost_estimate=pl.CostEstimate(flops=0, bytes_accessed=2 << 20, transcendentals=0),
    )(ids, *parts)


def back_kernel(ids, band, rows, spread, spill):
    me = ids[1]
    step = pl.program_id(0)

    @pl.when(step == 0)
    def _():
        for d in range(15):

            @pl.when(d < me)
            def _():
                spread[d] = jnp.zeros((32, 256), F32)

            @pl.when(d >= me)
            def _():
                spill[d] = jnp.zeros((32, 256), F32)

        spill[15] = jnp.zeros((32, 256), F32)

    for g in range(GROUP):
        i = step * GROUP + g
        value = jnp.dot(rows[i], band[g], preferred_element_type=F32)
        target = i + me

        @pl.when(target < 64)
        def _():
            spread[jnp.minimum(target, 63)] = value

        @pl.when(target >= 64)
        def _():
            spill[jnp.maximum(target - 64, 0)] = value


def band_back(ids, band, rows):
    return pl.pallas_call(
        back_kernel,
        grid_spec=pltpu.PrefetchScalarGridSpec(
            num_scalar_prefetch=1,
            grid=(64 // GROUP,),
            in_specs=[
                pl.BlockSpec((GROUP, 256, 256), lambda i, *_: (i, 0, 0)),
                whole((64, 32, 256)),
            ],
            out_specs=[whole((64, 32, 256)), whole((16, 32, 256))],
        ),
        out_shape=[
            jax.ShapeDtypeStruct((64, 32, 256), F32),
            jax.ShapeDtypeStruct((16, 32, 256), F32),
        ],
        compiler_params=params(),
        cost_estimate=pl.CostEstimate(
            flops=2 * 64 * 256 * 256 * 32, bytes_accessed=11 << 20, transcendentals=0
        ),
    )(ids, band, rows)


def far_kernel(ids, row_ids, col_ids, tiles, rows, base, c0, c1, c2, c3, out, k0, k1, k2, k3, cols, acc):
    mine, count = ids[0], ids[2]
    step = pl.program_id(0)

    @pl.when(step == 0)
    def _():
        out[...] = base[...]
        acc[...] = jnp.zeros_like(acc)
        for s in range(8):
            slot = mine ^ s
            for k, ref in enumerate((c0, c1, c2, c3)):

                @pl.when((slot & 3) == k)
                def _():
                    cols[4 * s : 4 * s + 4] = ref[slot >> 2]

    def both(g, i):
        a, b = row_ids[i], col_ids[i]
        forward = lax.dot_general(
            cols[b], tiles[g], (((1,), (1,)), ((), ())), preferred_element_type=F32
        )
        back = jnp.dot(rows[a], tiles[g], preferred_element_type=F32)
        return a, b, forward, back

    first = step * GROUP

    @pl.when(first + GROUP <= count)
    def _():
        found = [both(g, first + g) for g in range(GROUP)]
        for a, b, forward, back in found:
            out[a] += forward
            acc[b] += back

    @pl.when((first + GROUP > count) & (first < count))
    def _():
        for g in range(GROUP):

            @pl.when(first + g < count)
            def _():
                a, b, forward, back = both(g, first + g)
                out[a] += forward
                acc[b] += back

    @pl.when(step == pl.num_programs(0) - 1)
    def _():
        for j in range(8):
            source = mine ^ j
            (k0, k1, k2, k3)[j & 3][j >> 2] = acc[pl.ds(4 * source, 4)]


def far(ids, row_ids, col_ids, tiles, rows, base, parts):
    pair = (2, 4, 32, 256)
    return pl.pallas_call(
        far_kernel,
        grid_spec=pltpu.PrefetchScalarGridSpec(
            num_scalar_prefetch=3,
            grid=(64 // GROUP,),
            in_specs=[
                pl.BlockSpec((GROUP, 256, 256), lambda i, *_: (i, 0, 0)),
                whole((64, 32, 256)),
                whole((64, 32, 256)),
            ]
            + [whole(pair)] * 4,
            out_specs=[whole((64, 32, 256))] + [whole(pair)] * 4,
            scratch_shapes=[pltpu.VMEM((32, 32, 256), BF16), pltpu.VMEM((32, 32, 256), F32)],
        ),
        out_shape=[jax.ShapeDtypeStruct((64, 32, 256), F32)] + [jax.ShapeDtypeStruct(pair, F32)] * 4,
        compiler_params=params(),
        cost_estimate=pl.CostEstimate(
            flops=4 * 64 * 256 * 256 * 32, bytes_accessed=15 << 20, transcendentals=0
        ),
    )(ids, row_ids, col_ids, tiles, rows, base, *parts)


def forward_kernel(ids, band, rows, rim, base, spilled, same, other, extended):
    me = ids[1]
    step = pl.program_id(0)

    @pl.when(step == 0)
    def _():
        extended[:64] = rows[...]
        extended[64:80] = rim[...]

    for h in range(GROUP // 4):
        slab = step * (GROUP // 4) + h
        slot = me ^ slab
        total = []
        for t in range(4):
            i = slab * 4 + t
            product = lax.dot_general(
                extended[i + me], band[4 * h + t], (((1,), (1,)), ((), ())), preferred_element_type=F32
            )
            extra = jnp.where(i < 16, spilled[jnp.minimum(i, 15)], 0.0)
            total.append(product + base[i] + extra)

        @pl.when((slot & 1) == 0)
        def _():
            for t in range(4):
                same[slot >> 1, t] = total[t]

        @pl.when((slot & 1) == 1)
        def _():
            for t in range(4):
                other[slot >> 1, t] = total[t]


def band_forward(ids, band, rows, rim, base, spilled):
    return pl.pallas_call(
        forward_kernel,
        grid_spec=pltpu.PrefetchScalarGridSpec(
            num_scalar_prefetch=1,
            grid=(64 // GROUP,),
            in_specs=[
                pl.BlockSpec((GROUP, 256, 256), lambda i, *_: (i, 0, 0)),
                whole((64, 32, 256)),
                whole((16, 32, 256)),
                whole((64, 32, 256)),
                whole((16, 32, 256)),
            ],
            out_specs=[whole((8, 4, 32, 256))] * 2,
            scratch_shapes=[pltpu.VMEM((80, 32, 256), BF16)],
        ),
        out_shape=[jax.ShapeDtypeStruct((8, 4, 32, 256), F32)] * 2,
        compiler_params=params(),
        cost_estimate=pl.CostEstimate(
            flops=2 * 64 * 256 * 256 * 32, bytes_accessed=14 << 20, transcendentals=0
        ),
    )(ids, band, rows, rim, base, spilled)


def fold_kernel(same, arrived, *outs):
    for k in range(4):
        outs[k][...] = same[2 * k : 2 * k + 2] + arrived[2 * k : 2 * k + 2]


def fold(same, arrived):
    pair = jax.ShapeDtypeStruct((2, 4, 32, 256), F32)
    return pl.pallas_call(
        fold_kernel,
        out_shape=[pair] * 4,
        compiler_params=params(),
        cost_estimate=pl.CostEstimate(flops=0, bytes_accessed=3 << 20, transcendentals=0),
    )(same, arrived)


def against(left, right):
    return lax.dot_general(
        left, right, (((1,), (1,)), ((), ())), precision=PRECISE, preferred_element_type=F32
    )


def gram_kernel(n, with_images, *refs):
    basis, images = refs[: n + 1], refs[n + 1 : 2 * n + 1]
    terms = refs[2 * n + 1 : 2 * n + 5]
    mask, image_out, gram_out = refs[2 * n + 5 :]
    plain = jnp.zeros((32, 32 * (n + 1)), F32)
    cross = jnp.zeros((32, 32 * (n + 1)), F32)
    for t in range(4):
        image = ((terms[0][t] + terms[1][t]) + (terms[2][t] + terms[3][t])) * mask[t]
        image_out[t] = image
        newest = basis[-1][t]
        columns = jnp.concatenate([b[t] for b in basis], axis=0)
        plain += against(newest, columns)
        seen = jnp.concatenate([b[t] for b in images] + [image], axis=0)
        cross += 0.5 * (against(newest, seen) + against(image, columns))
    gram_out[...] = jnp.concatenate([plain, cross], axis=1)


def grams(older, older_images, newest, terms, mask):
    n = len(older)
    return pl.pallas_call(
        functools.partial(gram_kernel, n, True),
        out_shape=[
            jax.ShapeDtypeStruct((4, 32, 256), F32),
            jax.ShapeDtypeStruct((32, 64 * (n + 1)), F32),
        ],
        compiler_params=params(),
        cost_estimate=pl.CostEstimate(flops=1 << 27, bytes_accessed=1 << 20, transcendentals=0),
    )(*older, newest, *older_images, *terms, mask)


def mul(left, right):
    return jnp.dot(left, right, precision=PRECISE, preferred_element_type=F32)


def update_kernel(n, last, *refs):
    basis, images = refs[:n], refs[n : 2 * n]
    weights, ritz, mask = refs[2 * n : 2 * n + 3]
    outs = refs[2 * n + 3 :]
    for t in range(4):
        moved = mul(weights[...], jnp.concatenate([b[t] for b in basis], axis=0))
        outs[0][t] = moved[:32]
        if last:
            continue
        moved_images = mul(weights[...], jnp.concatenate([b[t] for b in images], axis=0))
        outs[1][t] = moved_images[:32]
        residual = moved_images[:32] - mul(ritz[...], moved[:32])
        outs[2][t] = residual
        outs[3][t] = (residual * mask[t]).astype(BF16)
        if moved.shape[0] > 32:
            outs[4][t] = moved[32:]
            outs[5][t] = moved_images[32:]


def update(basis, images, weights, ritz, mask, last=False):
    n = len(basis)
    slab = jax.ShapeDtypeStruct((4, 32, 256), F32)
    outs = [slab] if last else [slab, slab, slab, jax.ShapeDtypeStruct((4, 32, 256), BF16)]
    if not last and weights.shape[0] > 32:
        outs += [slab, slab]
    return pl.pallas_call(
        functools.partial(update_kernel, n, last),
        out_shape=outs,
        compiler_params=params(),
        cost_estimate=pl.CostEstimate(flops=1 << 27, bytes_accessed=1 << 20, transcendentals=0),
    )(*basis, *images, weights, ritz, mask)


def symmetric(matrix):
    return 0.5 * (matrix + matrix.T)


def right_solve(values, factor):
    return lax.linalg.triangular_solve(
        factor, values, left_side=False, lower=True, transpose_a=True
    )


def left_solve(factor, values, transposed):
    return lax.linalg.triangular_solve(
        factor, values, left_side=True, lower=True, transpose_a=transposed
    )


def rayleigh_ritz(basis_gram, image_gram, block_width):
    factor = jnp.linalg.cholesky(basis_gram)
    reduced = symmetric(right_solve(left_solve(factor, image_gram, False), factor))
    order = reduced.shape[0]
    scaling = jnp.sqrt(jnp.sum(reduced * reduced))
    filtered = (reduced + scaling * jnp.eye(order, dtype=F32)) / (2.0 * scaling)
    filtered = mul(filtered, filtered)
    filtered = mul(filtered, filtered)
    leading = filtered[:, :block_width]
    small_factor = jnp.linalg.cholesky(mul(leading.T, leading))
    orthonormal = right_solve(leading, small_factor)
    return left_solve(factor, orthonormal, True)


def grown(known, row):
    edge = row[:, : known.shape[0]]
    return jnp.concatenate(
        [
            jnp.concatenate([known, edge.T], axis=1),
            jnp.concatenate([edge, symmetric(row[:, known.shape[0] :])], axis=1),
        ],
        axis=0,
    )


def body(x_start, bin_mask, band, off_tiles, off_rows, off_cols, off_count):
    width = x_start.shape[1]
    band = band[:, 0]
    tiles = off_tiles[0, 0]
    row_ids, col_ids = off_rows[0, 0], off_cols[0, 0]
    ids = jnp.stack(
        [lax.axis_index("brow"), lax.axis_index("bcol"), off_count[0, 0], jnp.int32(0)]
    ).astype(jnp.int32)
    mask = bin_mask.astype(F32).reshape(4, 1, 256)
    started = x_start.T.reshape(width, 4, 256).transpose(1, 0, 2) * mask

    def apply_operator(packed):
        pair = jnp.stack([packed, flip(packed, "bcol", 2)])
        near = [pair] + [flip(pair, "bcol", 4 * k) for k in (1, 2, 3)]
        across = [flip(part, "bcol", 1) for part in near]
        col_pair = jnp.stack([packed, flip(packed, "brow", 4)])
        col_parts = [col_pair] + [flip(col_pair, "brow", k) for k in (1, 2, 3)]
        rows, rim = assemble(ids, near + across)
        rim = shifted(rim, "brow", -1)
        spread, spill = band_back(ids, band, rows)
        spilled = shifted(spill, "brow", 1)
        base, *col_sums = far(ids, row_ids, col_ids, tiles, rows, spread, col_parts)
        c0, c1, c2, c3 = [col_sums[0]] + [flip(col_sums[k], "brow", k) for k in (1, 2, 3)]
        col_total = (c0 + c1) + (c2 + c3)
        col_other = flip(col_total[1], "brow", 4)
        same, other = band_forward(ids, band, rows, rim, base, spilled)
        folded = fold(same, flip(other, "bcol", 1))
        r0, r1, r2, r3 = [folded[0]] + [flip(folded[k], "bcol", 4 * k) for k in (1, 2, 3)]
        row_total = (r0 + r1) + (r2 + r3)
        row_other = flip(row_total[1], "bcol", 2)
        return [row_total[0], row_other, col_total[0], col_other]

    terms = apply_operator((started * mask).astype(BF16))
    image, gram = grams([], [], started, terms, mask)
    gram = sum_all(gram)
    start_gram, start_images = symmetric(gram[:, :width]), symmetric(gram[:, width:])
    factor = jnp.linalg.cholesky(start_gram)
    inverse = left_solve(factor, jnp.eye(width, dtype=F32), False)
    ritz = symmetric(mul(mul(inverse, start_images), inverse.T))
    known_basis, known_images = symmetric(mul(mul(inverse, start_gram), inverse.T)), ritz
    vectors, images, residual, packed = update([started], [image], inverse, ritz, mask)
    older, older_images = [vectors], [images]
    for step in range(STEPS):
        terms = apply_operator(packed)
        residual_image, gram = grams(older, older_images, residual, terms, mask)
        gram = sum_all(gram)
        order = width * (len(older) + 1)
        basis_gram = grown(known_basis, gram[:, :order])
        image_gram = grown(known_images, gram[:, order:])
        scaling = lax.rsqrt(jnp.diagonal(basis_gram)[width:] + EPSILON)
        scaling = jnp.concatenate([jnp.ones((width,), F32), scaling])
        weights = scaling[:, None] * rayleigh_ritz(
            scaling[:, None] * basis_gram * scaling[None, :],
            scaling[:, None] * image_gram * scaling[None, :],
            width,
        )
        tail = jnp.concatenate([jnp.zeros((width, width), F32), weights[width:]], axis=0)
        both = jnp.concatenate([weights, tail], axis=1)
        known_images = symmetric(mul(both.T, mul(image_gram, both)))
        ritz = known_images[:width, :width]
        basis, basis_images = older + [residual], older_images + [residual_image]
        if step == STEPS - 1:
            (vectors,) = update(basis, basis_images, weights.T, ritz, mask, last=True)
        else:
            known_basis = symmetric(mul(both.T, mul(basis_gram, both)))
            vectors, images, residual, packed, previous, previous_images = update(
                basis, basis_images, both.T, ritz, mask
            )
            older, older_images = [vectors, previous], [images, previous_images]
    return vectors.transpose(1, 0, 2).reshape(width, -1).T, ritz


def solution(mesh):
    return jax.shard_map(
        body,
        mesh=mesh,
        in_specs=(
            P(("brow", "bcol"), None),
            P(("brow", "bcol")),
            P("brow", "bcol", None, None),
            P("brow", "bcol", None, None, None),
            P("brow", "bcol", None),
            P("brow", "bcol", None),
            P("brow", "bcol"),
        ),
        out_specs=(P(("brow", "bcol"), None), P()),
        check_vma=False,
    )
```

time: 1550 us -> 612 us (0.39)
  blocking collectives: 745 us -> 0 us
  waiting for transfers between devices: 491 us -> 197 us
  starting transfers between devices: 19.9 us -> 177 us
  Pallas kernels: 0 us -> 112 us
  matrix products: 93 us -> 7.77 us
  other arithmetic: 143 us -> 80.5 us
    psum x9 -> x0, blocking collectives: 601 us -> none  [global_sum(): return lax.psum(parts, ('brow', 'bcol'))]
    psum x2 -> x0, waiting for transfers between devices: 277 us -> none  [global_sum(): return lax.psum(parts, ('brow', 'bcol'))]
    ppermute x0 -> x124, waiting for transfers between devices: none -> 197 us  [the longest x120 191 us: flip(): return lax.ppermute(value, axis, [(i, i ^ by) for i in range(length)])]
    ppermute x0 -> x124, starting transfers between devices: none -> 158 us  [the longest x120 145 us: flip(): return lax.ppermute(value, axis, [(i, i ^ by) for i in range(length)])]
    all_gather x4 -> x0, blocking collectives: 144 us -> none  [operator_core(): col_b = lax.all_gather(slab_b, 'brow', axis=0, tiled=True)]
    reduce_scatter x8 -> x0, waiting for transfers between devices: 113 us -> none  [the longest x4 107 us: operator_core(): lax.psum_scatter(own_rows.reshape(-1, block_width), 'bcol', scatter_dimen...]
    pallas_call x0 -> x28, Pallas kernels: none -> 112 us  [the longest x4 42.4 us: band_back(): pl.pallas_call(back_kernel, grid_spec=pltpu.PrefetchScalarGridSpec(num_sc...]
    all_gather x4 -> x0, waiting for transfers between devices: 88.7 us -> none  [apply_operator(): row_b = lax.all_gather(slab_b, 'bcol', axis=0, tiled=True)]
  transfers between devices with their start and end apart: 22 -> 132, of which waited for: 14 -> 88; matrix products, arithmetic and copies ran while one was open for 7% -> 1% of each run, Pallas kernels for 0% -> 6%
where the time goes in v1:
time: 612 us; the launch traced here: 602 us
  waiting for transfers between devices  197 us (32%)
  starting transfers between devices  177 us (29%)
  Pallas kernels  112 us (18%)
  other arithmetic  80.5 us (13%)
  local copies, waits for them, and re-layouts  22.5 us (4%)
  matrix products  7.77 us (1%)
    ppermute x120, waiting for transfers between devices, flip(): return lax.ppermute(value, axis, [(i, i ^ by) for i in range(length)])  191 us
    ppermute x120, starting transfers between devices, flip(): return lax.ppermute(value, axis, [(i, i ^ by) for i in range(length)])  145 us
    pallas_call x4, Pallas kernels, band_back(): pl.pallas_call(back_kernel, grid_spec=pltpu.PrefetchScalarGridSpec(num_sc...  42.4 us
    pallas_call x4, Pallas kernels, far(): pl.pallas_call(far_kernel, grid_spec=pltpu.PrefetchScalarGridSpec(num_sca...  37.6 us
    another operation x9, other arithmetic, rayleigh_ritz(): factor = jnp.linalg.cholesky(basis_gram)  25.4 us
    another operation x8, other arithmetic, left_solve(): lax.linalg.triangular_solve(factor, values, left_side=True, lower=True, t...  24.7 us
    pallas_call x4, Pallas kernels, band_forward(): pl.pallas_call(forward_kernel, grid_spec=pltpu.PrefetchScalarGridSpec(num...  20.3 us
    ppermute x8, starting transfers between devices, shifted(): return lax.ppermute(value, axis, pairs)  19 us
  transfers between devices with their start and end apart: 132, of which 88 were waited for; matrix products, arithmetic and copies ran while one was open for 1% of the time, Pallas kernels for 6%

profile of v1, /device:TPU:0, one launch (start us, length us, event | category | flops | bytes accessed | tf_op | source)
XLA Modules:
  0.0 602.3 jit_solution(13310934318720781500)
XLA Ops:
  26.0 10.6 %shard_map.87 = (f32[64,32,256]{2,1,0:T(8,128)S(1)}, f32[16,32,256]{2,1,0:T(8,128)S(1)}) custom-call(s32[4]{0:T(128)S(1)} %pad_add_fusion.ids, bf16[64,256,256]{2,1,0:T(8,128)(2,1)S(1)} %bitcast.292, bf16[64,32,256]{2,1,0:T(8,128)(2,1)S(1)} %get-tuple-element.92.rows), custom_call_target="tpu_custom_call" | custom-call | flops 268435456 | bytes 11534336 | tf_op jit(solution)/shard_map/pallas_call | solution.py:120
  36.6 3.9 collective-permute-start.13
  41.7 4.8 collective-permute-start.12
  47.5 10.2 %collective-permute-done.12.c3 = bf16[2,4,32,256]{3,2,1,0:T(8,128)(2,1)S(1)} collective-permute-done((bf16[2,4,32,256]{3,2,1,0:T(8,128)(2,1)S(1)}, bf16[2,4,32,256]{3,2,1,0:T(8,128)(2,1)S(1)}, u32[]{:S(2)}, u32[]{:S(2)}) %collective-permute-start.12) | collective-permute-done | bytes 131104 | tf_op jit(solution)/shard_map/ppermute | solution.py:21
  59.5 9.4 %shard_map.88 = (f32[64,32,256]{2,1,0:T(8,128)S(1)}, f32[2,4,32,256]{3,2,1,0:T(8,128)S(1)}, f32[2,4,32,256]{3,2,1,0:T(8,128)S(1)}, f32[2,4,32,256]{3,2,1,0:T(8,128)S(1)}, f32[2,4,32,256]{3,2,1,0:T(8,128)S(1)}) custom-call(s32[4]{0:T(128)S(1)} %pad_add_fusion.ids, s32[64]{0:T(128)S(1)} %bitcast.321, s32[64]{0:T(128)S(1)} %bitcast.325, ...), custom_call_target="tpu_custom_call" | custom-call | flops 536870912 | bytes 15728640 | tf_op jit(solution)/shard_map/pallas_call | solution.py:194
  69.0 5.1 shard_map.89
  84.6 6.0 collective-permute-done.20
  156.7 10.6 %shard_map.94 = (f32[64,32,256]{2,1,0:T(8,128)S(1)}, f32[16,32,256]{2,1,0:T(8,128)S(1)}) custom-call(s32[4]{0:T(128)S(1)} %pad_add_fusion.ids, bf16[64,256,256]{2,1,0:T(8,128)(2,1)S(1)} %bitcast.296, bf16[64,32,256]{2,1,0:T(8,128)(2,1)S(1)} %get-tuple-element.113.rows), custom_call_target="tpu_custom_call" | custom-call | flops 268435456 | bytes 11534336 | tf_op jit(solution)/shard_map/pallas_call | solution.py:120
  167.3 3.6 collective-permute-start.46
  177.0 10.0 %collective-permute-done.45.c3 = bf16[2,4,32,256]{3,2,1,0:T(8,128)(2,1)S(1)} collective-permute-done((bf16[2,4,32,256]{3,2,1,0:T(8,128)(2,1)S(1)}, bf16[2,4,32,256]{3,2,1,0:T(8,128)(2,1)S(1)}, u32[]{:S(2)}, u32[]{:S(2)}) %collective-permute-start.45) | collective-permute-done | bytes 131104 | tf_op jit(solution)/shard_map/ppermute | solution.py:21
  188.5 9.4 %shard_map.95 = (f32[64,32,256]{2,1,0:T(8,128)S(1)}, f32[2,4,32,256]{3,2,1,0:T(8,128)S(1)}, f32[2,4,32,256]{3,2,1,0:T(8,128)S(1)}, f32[2,4,32,256]{3,2,1,0:T(8,128)S(1)}, f32[2,4,32,256]{3,2,1,0:T(8,128)S(1)}) custom-call(s32[4]{0:T(128)S(1)} %pad_add_fusion.ids, s32[64]{0:T(128)S(1)} %bitcast.322, s32[64]{0:T(128)S(1)} %bitcast.326, ...), custom_call_target="tpu_custom_call" | custom-call | flops 536870912 | bytes 15728640 | tf_op jit(solution)/shard_map/pallas_call | solution.py:194
  198.0 5.1 shard_map.96
  213.8 5.5 collective-permute-done.53
  228.6 3.6 collective-permute-done.51.refs_4_
  261.5 5.8 cholesky.58
  268.7 4.9 custom-call.33
  306.9 10.6 %shard_map.101 = (f32[64,32,256]{2,1,0:T(8,128)S(1)}, f32[16,32,256]{2,1,0:T(8,128)S(1)}) custom-call(s32[4]{0:T(128)S(1)} %pad_add_fusion.ids, bf16[64,256,256]{2,1,0:T(8,128)(2,1)S(1)} %bitcast.300, bf16[64,32,256]{2,1,0:T(8,128)(2,1)S(1)} %get-tuple-element.136.rows), custom_call_target="tpu_custom_call" | custom-call | flops 268435456 | bytes 11534336 | tf_op jit(solution)/shard_map/pallas_call | solution.py:120
  327.1 10.0 %collective-permute-done.78.c3 = bf16[2,4,32,256]{3,2,1,0:T(8,128)(2,1)S(1)} collective-permute-done((bf16[2,4,32,256]{3,2,1,0:T(8,128)(2,1)S(1)}, bf16[2,4,32,256]{3,2,1,0:T(8,128)(2,1)S(1)}, u32[]{:S(2)}, u32[]{:S(2)}) %collective-permute-start.78) | collective-permute-done | bytes 131104 | tf_op jit(solution)/shard_map/ppermute | solution.py:21
  338.4 9.4 %shard_map.102 = (f32[64,32,256]{2,1,0:T(8,128)S(1)}, f32[2,4,32,256]{3,2,1,0:T(8,128)S(1)}, f32[2,4,32,256]{3,2,1,0:T(8,128)S(1)}, f32[2,4,32,256]{3,2,1,0:T(8,128)S(1)}, f32[2,4,32,256]{3,2,1,0:T(8,128)S(1)}) custom-call(s32[4]{0:T(128)S(1)} %pad_add_fusion.ids, s32[64]{0:T(128)S(1)} %bitcast.323, s32[64]{0:T(128)S(1)} %bitcast.327, ...), custom_call_target="tpu_custom_call" | custom-call | flops 536870912 | bytes 15728640 | tf_op jit(solution)/shard_map/pallas_call | solution.py:194
  347.9 5.1 shard_map.103
  363.7 5.6 collective-permute-done.86
  414.2 8.8 %cholesky.175 = f32[96,96]{1,0:T(8,128)S(1)} custom-call(f32[96,96]{1,0:T(8,128)S(1)} %copy.135), custom_call_target="Cholesky" | custom-call | tf_op jit(solution)/shard_map/jit(cholesky)/cholesky | solution.py:377
  424.4 7.4 %custom-call.48 = f32[1,96,96]{1,2,0:T(8,128)S(1)} custom-call(f32[1,96,96]{2,1,0:T(8,128)S(1)} %fusion.1), custom_call_target="InvertDiagBlocksLowerTriangular" | custom-call | tf_op jit(solution)/shard_map/triangular_solve/custom-call.11 | solution.py:371
  465.6 10.6 %shard_map.108 = (f32[64,32,256]{2,1,0:T(8,128)S(1)}, f32[16,32,256]{2,1,0:T(8,128)S(1)}) custom-call(s32[4]{0:T(128)S(1)} %pad_add_fusion.ids, bf16[64,256,256]{2,1,0:T(8,128)(2,1)S(1)} %bitcast.304, bf16[64,32,256]{2,1,0:T(8,128)(2,1)S(1)} %get-tuple-element.159.rows), custom_call_target="tpu_custom_call" | custom-call | flops 268435456 | bytes 11534336 | tf_op jit(solution)/shard_map/pallas_call | solution.py:120
  480.4 3.9 collective-permute-start.111
  485.5 10.1 %collective-permute-done.111.c3 = bf16[2,4,32,256]{3,2,1,0:T(8,128)(2,1)S(1)} collective-permute-done((bf16[2,4,32,256]{3,2,1,0:T(8,128)(2,1)S(1)}, bf16[2,4,32,256]{3,2,1,0:T(8,128)(2,1)S(1)}, u32[]{:S(2)}, u32[]{:S(2)}) %collective-permute-start.111) | collective-permute-done | bytes 131104 | tf_op jit(solution)/shard_map/ppermute | solution.py:21
  496.7 9.4 %shard_map.109 = (f32[64,32,256]{2,1,0:T(8,128)S(1)}, f32[2,4,32,256]{3,2,1,0:T(8,128)S(1)}, f32[2,4,32,256]{3,2,1,0:T(8,128)S(1)}, f32[2,4,32,256]{3,2,1,0:T(8,128)S(1)}, f32[2,4,32,256]{3,2,1,0:T(8,128)S(1)}) custom-call(s32[4]{0:T(128)S(1)} %pad_add_fusion.ids, s32[64]{0:T(128)S(1)} %bitcast.324, s32[64]{0:T(128)S(1)} %bitcast.328, ...), custom_call_target="tpu_custom_call" | custom-call | flops 536870912 | bytes 15728640 | tf_op jit(solution)/shard_map/pallas_call | solution.py:194
  506.2 5.1 shard_map.110
  522.0 5.6 collective-permute-done.119
  530.2 3.8 collective-permute-start.121
  572.8 8.8 %cholesky.197 = f32[96,96]{1,0:T(8,128)S(1)} custom-call(f32[96,96]{1,0:T(8,128)S(1)} %copy.147), custom_call_target="Cholesky" | custom-call | tf_op jit(solution)/shard_map/jit(cholesky)/cholesky | solution.py:377
  582.9 7.4 %custom-call.52 = f32[1,96,96]{1,2,0:T(8,128)S(1)} custom-call(f32[1,96,96]{2,1,0:T(8,128)S(1)} %fusion.2), custom_call_target="InvertDiagBlocksLowerTriangular" | custom-call | tf_op jit(solution)/shard_map/triangular_solve/custom-call.11 | solution.py:371
  (530 shorter events, 367.1 us)
Async XLA Ops:
  36.6 32.4 %collective-permute-start.13 = (f32[16,32,256]{2,1,0:T(8,128)S(1)}, f32[16,32,256]{2,1,0:T(8,128)S(1)}, u32[]{:S(2)}, u32[]{:S(2)}) collective-permute-start(f32[16,32,256]{2,1,0:T(8,128)S(1)} %get-tuple-element.96), channel_id=1, source_target_pairs={{0,16},{16,32},{32,48},{48,64},{64,80},{80,96},{96,112},{1,17},{17... | collective-permute-start | bytes 1572872 | tf_op jit(solution)/shard_map/ppermute | solution.py:35
  40.4 28.5 %collective-permute-start.8 = (bf16[16,32,256]{2,1,0:T(8,128)(2,1)S(1)}, bf16[16,32,256]{2,1,0:T(8,128)(2,1)S(1)}, u32[]{:S(2)}, u32[]{:S(2)}) collective-permute-start(bf16[16,32,256]{2,1,0:T(8,128)(2,1)S(1)} %get-tuple-element.93), channel_id=1, source_target_pairs={{16,0},{32,16},{48,32},{64,48},{80,64},{96,80},{112,96},{17,1},{33... | collective-permute-start | bytes 786440 | tf_op jit(solution)/shard_map/ppermute | solution.py:35
  41.7 16.0 %collective-permute-start.12 = (bf16[2,4,32,256]{3,2,1,0:T(8,128)(2,1)S(1)}, bf16[2,4,32,256]{3,2,1,0:T(8,128)(2,1)S(1)}, u32[]{:S(2)}, u32[]{:S(2)}) collective-permute-start(bf16[2,4,32,256]{3,2,1,0:T(8,128)(2,1)S(1)} %get-tuple-element.216.c0), channel_id=1, source_target_pairs={{0,48},{16,32},{32,16},{48,0},{64,112},{80,96},{96,80},{112,64},{1... | collective-permute-start | bytes 393224 | tf_op jit(solution)/shard_map/ppermute | solution.py:21
  74.7 15.9 %collective-permute-start.20 = (f32[2,4,32,256]{3,2,1,0:T(8,128)S(1)}, f32[2,4,32,256]{3,2,1,0:T(8,128)S(1)}, u32[]{:S(2)}, u32[]{:S(2)}) collective-permute-start(f32[2,4,32,256]{3,2,1,0:T(8,128)S(1)} %get-tuple-element.105), channel_id=1, source_target_pairs={{0,32},{16,48},{32,0},{48,16},{64,96},{80,112},{96,64},{112,80},{1... | collective-permute-start | bytes 786440 | tf_op jit(solution)/shard_map/ppermute | solution.py:21
  78.2 14.9 %collective-permute-start.21 = (f32[2,4,32,256]{3,2,1,0:T(8,128)S(1)}, f32[2,4,32,256]{3,2,1,0:T(8,128)S(1)}, u32[]{:S(2)}, u32[]{:S(2)}) collective-permute-start(f32[2,4,32,256]{3,2,1,0:T(8,128)S(1)} %get-tuple-element.106), channel_id=1, source_target_pairs={{0,48},{16,32},{32,16},{48,0},{64,112},{80,96},{96,80},{112,64},{1... | collective-permute-start | bytes 786440 | tf_op jit(solution)/shard_map/ppermute | solution.py:21
  79.1 16.3 %collective-permute-start.15 = (f32[2,4,32,256]{3,2,1,0:T(8,128)S(1)}, f32[2,4,32,256]{3,2,1,0:T(8,128)S(1)}, u32[]{:S(2)}, u32[]{:S(2)}) collective-permute-start(f32[2,4,32,256]{3,2,1,0:T(8,128)S(1)} %get-tuple-element.100), channel_id=1, source_target_pairs={{0,4},{1,5},{2,6},{3,7},{4,0},{5,1},{6,2},{7,3},{8,12},{9,13},{10,... | collective-permute-start | bytes 786440 | tf_op jit(solution)/shard_map/ppermute | solution.py:21
  79.6 15.8 %collective-permute-start.16 = (f32[2,4,32,256]{3,2,1,0:T(8,128)S(1)}, f32[2,4,32,256]{3,2,1,0:T(8,128)S(1)}, u32[]{:S(2)}, u32[]{:S(2)}) collective-permute-start(f32[2,4,32,256]{3,2,1,0:T(8,128)S(1)} %get-tuple-element.101), channel_id=1, source_target_pairs={{0,8},{1,9},{2,10},{3,11},{4,12},{5,13},{6,14},{7,15},{8,0},{9,1},... | collective-permute-start | bytes 786440 | tf_op jit(solution)/shard_map/ppermute | solution.py:21
  83.4 14.1 %collective-permute-start.17 = (f32[2,4,32,256]{3,2,1,0:T(8,128)S(1)}, f32[2,4,32,256]{3,2,1,0:T(8,128)S(1)}, u32[]{:S(2)}, u32[]{:S(2)}) collective-permute-start(f32[2,4,32,256]{3,2,1,0:T(8,128)S(1)} %get-tuple-element.102), channel_id=1, source_target_pairs={{0,12},{1,13},{2,14},{3,15},{4,8},{5,9},{6,10},{7,11},{8,4},{9,5},... | collective-permute-start | bytes 786440 | tf_op jit(solution)/shard_map/ppermute | solution.py:21
  167.3 30.7 %collective-permute-start.46 = (f32[16,32,256]{2,1,0:T(8,128)S(1)}, f32[16,32,256]{2,1,0:T(8,128)S(1)}, u32[]{:S(2)}, u32[]{:S(2)}) collective-permute-start(f32[16,32,256]{2,1,0:T(8,128)S(1)} %get-tuple-element.117), channel_id=1, source_target_pairs={{0,16},{16,32},{32,48},{48,64},{64,80},{80,96},{96,112},{1,17},{17... | collective-permute-start | bytes 1572872 | tf_op jit(solution)/shard_map/ppermute | solution.py:35
  170.9 27.0 %collective-permute-start.41 = (bf16[16,32,256]{2,1,0:T(8,128)(2,1)S(1)}, bf16[16,32,256]{2,1,0:T(8,128)(2,1)S(1)}, u32[]{:S(2)}, u32[]{:S(2)}) collective-permute-start(bf16[16,32,256]{2,1,0:T(8,128)(2,1)S(1)} %get-tuple-element.114), channel_id=1, source_target_pairs={{16,0},{32,16},{48,32},{64,48},{80,64},{96,80},{112,96},{17,1},{33... | collective-permute-start | bytes 786440 | tf_op jit(solution)/shard_map/ppermute | solution.py:35
  172.2 14.8 %collective-permute-start.45 = (bf16[2,4,32,256]{3,2,1,0:T(8,128)(2,1)S(1)}, bf16[2,4,32,256]{3,2,1,0:T(8,128)(2,1)S(1)}, u32[]{:S(2)}, u32[]{:S(2)}) collective-permute-start(bf16[2,4,32,256]{3,2,1,0:T(8,128)(2,1)S(1)} %get-tuple-element.214.c0), channel_id=1, source_target_pairs={{0,48},{16,32},{32,16},{48,0},{64,112},{80,96},{96,80},{112,64},{1... | collective-permute-start | bytes 393224 | tf_op jit(solution)/shard_map/ppermute | solution.py:21
  205.0 14.4 %collective-permute-start.53 = (f32[2,4,32,256]{3,2,1,0:T(8,128)S(1)}, f32[2,4,32,256]{3,2,1,0:T(8,128)S(1)}, u32[]{:S(2)}, u32[]{:S(2)}) collective-permute-start(f32[2,4,32,256]{3,2,1,0:T(8,128)S(1)} %get-tuple-element.126), channel_id=1, source_target_pairs={{0,32},{16,48},{32,0},{48,16},{64,96},{80,112},{96,64},{112,80},{1... | collective-permute-start | bytes 786440 | tf_op jit(solution)/shard_map/ppermute | solution.py:21
  207.0 14.9 %collective-permute-start.54 = (f32[2,4,32,256]{3,2,1,0:T(8,128)S(1)}, f32[2,4,32,256]{3,2,1,0:T(8,128)S(1)}, u32[]{:S(2)}, u32[]{:S(2)}) collective-permute-start(f32[2,4,32,256]{3,2,1,0:T(8,128)S(1)} %get-tuple-element.127), channel_id=1, source_target_pairs={{0,48},{16,32},{32,16},{48,0},{64,112},{80,96},{96,80},{112,64},{1... | collective-permute-start | bytes 786440 | tf_op jit(solution)/shard_map/ppermute | solution.py:21
  208.1 17.4 %collective-permute-start.48 = (f32[2,4,32,256]{3,2,1,0:T(8,128)S(1)}, f32[2,4,32,256]{3,2,1,0:T(8,128)S(1)}, u32[]{:S(2)}, u32[]{:S(2)}) collective-permute-start(f32[2,4,32,256]{3,2,1,0:T(8,128)S(1)} %get-tuple-element.121), channel_id=1, source_target_pairs={{0,4},{1,5},{2,6},{3,7},{4,0},{5,1},{6,2},{7,3},{8,12},{9,13},{10,... | collective-permute-start | bytes 786440 | tf_op jit(solution)/shard_map/ppermute | solution.py:21
  208.8 16.6 %collective-permute-start.49 = (f32[2,4,32,256]{3,2,1,0:T(8,128)S(1)}, f32[2,4,32,256]{3,2,1,0:T(8,128)S(1)}, u32[]{:S(2)}, u32[]{:S(2)}) collective-permute-start(f32[2,4,32,256]{3,2,1,0:T(8,128)S(1)} %get-tuple-element.122), channel_id=1, source_target_pairs={{0,8},{1,9},{2,10},{3,11},{4,12},{5,13},{6,14},{7,15},{8,0},{9,1},... | collective-permute-start | bytes 786440 | tf_op jit(solution)/shard_map/ppermute | solution.py:21
  212.4 14.2 %collective-permute-start.50 = (f32[2,4,32,256]{3,2,1,0:T(8,128)S(1)}, f32[2,4,32,256]{3,2,1,0:T(8,128)S(1)}, u32[]{:S(2)}, u32[]{:S(2)}) collective-permute-start(f32[2,4,32,256]{3,2,1,0:T(8,128)S(1)} %get-tuple-element.123), channel_id=1, source_target_pairs={{0,12},{1,13},{2,14},{3,15},{4,8},{5,9},{6,10},{7,11},{8,4},{9,5},... | collective-permute-start | bytes 786440 | tf_op jit(solution)/shard_map/ppermute | solution.py:21
  317.5 30.3 %collective-permute-start.79 = (f32[16,32,256]{2,1,0:T(8,128)S(1)}, f32[16,32,256]{2,1,0:T(8,128)S(1)}, u32[]{:S(2)}, u32[]{:S(2)}) collective-permute-start(f32[16,32,256]{2,1,0:T(8,128)S(1)} %get-tuple-element.140), channel_id=1, source_target_pairs={{0,16},{16,32},{32,48},{48,64},{64,80},{80,96},{96,112},{1,17},{17... | collective-permute-start | bytes 1572872 | tf_op jit(solution)/shard_map/ppermute | solution.py:35
  321.0 26.9 %collective-permute-start.74 = (bf16[16,32,256]{2,1,0:T(8,128)(2,1)S(1)}, bf16[16,32,256]{2,1,0:T(8,128)(2,1)S(1)}, u32[]{:S(2)}, u32[]{:S(2)}) collective-permute-start(bf16[16,32,256]{2,1,0:T(8,128)(2,1)S(1)} %get-tuple-element.137), channel_id=1, source_target_pairs={{16,0},{32,16},{48,32},{64,48},{80,64},{96,80},{112,96},{17,1},{33... | collective-permute-start | bytes 786440 | tf_op jit(solution)/shard_map/ppermute | solution.py:35
  322.3 14.8 %collective-permute-start.78 = (bf16[2,4,32,256]{3,2,1,0:T(8,128)(2,1)S(1)}, bf16[2,4,32,256]{3,2,1,0:T(8,128)(2,1)S(1)}, u32[]{:S(2)}, u32[]{:S(2)}) collective-permute-start(bf16[2,4,32,256]{3,2,1,0:T(8,128)(2,1)S(1)} %get-tuple-element.206.c0), channel_id=1, source_target_pairs={{0,48},{16,32},{32,16},{48,0},{64,112},{80,96},{96,80},{112,64},{1... | collective-permute-start | bytes 393224 | tf_op jit(solution)/shard_map/ppermute | solution.py:21
  354.9 14.4 %collective-permute-start.86 = (f32[2,4,32,256]{3,2,1,0:T(8,128)S(1)}, f32[2,4,32,256]{3,2,1,0:T(8,128)S(1)}, u32[]{:S(2)}, u32[]{:S(2)}) collective-permute-start(f32[2,4,32,256]{3,2,1,0:T(8,128)S(1)} %get-tuple-element.149), channel_id=1, source_target_pairs={{0,32},{16,48},{32,0},{48,16},{64,96},{80,112},{96,64},{112,80},{1... | collective-permute-start | bytes 786440 | tf_op jit(solution)/shard_map/ppermute | solution.py:21
  356.9 14.9 %collective-permute-start.87 = (f32[2,4,32,256]{3,2,1,0:T(8,128)S(1)}, f32[2,4,32,256]{3,2,1,0:T(8,128)S(1)}, u32[]{:S(2)}, u32[]{:S(2)}) collective-permute-start(f32[2,4,32,256]{3,2,1,0:T(8,128)S(1)} %get-tuple-element.150), channel_id=1, source_target_pairs={{0,48},{16,32},{32,16},{48,0},{64,112},{80,96},{96,80},{112,64},{1... | collective-permute-start | bytes 786440 | tf_op jit(solution)/shard_map/ppermute | solution.py:21
  358.0 17.4 %collective-permute-start.81 = (f32[2,4,32,256]{3,2,1,0:T(8,128)S(1)}, f32[2,4,32,256]{3,2,1,0:T(8,128)S(1)}, u32[]{:S(2)}, u32[]{:S(2)}) collective-permute-start(f32[2,4,32,256]{3,2,1,0:T(8,128)S(1)} %get-tuple-element.144), channel_id=1, source_target_pairs={{0,4},{1,5},{2,6},{3,7},{4,0},{5,1},{6,2},{7,3},{8,12},{9,13},{10,... | collective-permute-start | bytes 786440 | tf_op jit(solution)/shard_map/ppermute | solution.py:21
  358.7 16.6 %collective-permute-start.82 = (f32[2,4,32,256]{3,2,1,0:T(8,128)S(1)}, f32[2,4,32,256]{3,2,1,0:T(8,128)S(1)}, u32[]{:S(2)}, u32[]{:S(2)}) collective-permute-start(f32[2,4,32,256]{3,2,1,0:T(8,128)S(1)} %get-tuple-element.145), channel_id=1, source_target_pairs={{0,8},{1,9},{2,10},{3,11},{4,12},{5,13},{6,14},{7,15},{8,0},{9,1},... | collective-permute-start | bytes 786440 | tf_op jit(solution)/shard_map/ppermute | solution.py:21
  362.3 14.2 %collective-permute-start.83 = (f32[2,4,32,256]{3,2,1,0:T(8,128)S(1)}, f32[2,4,32,256]{3,2,1,0:T(8,128)S(1)}, u32[]{:S(2)}, u32[]{:S(2)}) collective-permute-start(f32[2,4,32,256]{3,2,1,0:T(8,128)S(1)} %get-tuple-element.146), channel_id=1, source_target_pairs={{0,12},{1,13},{2,14},{3,15},{4,8},{5,9},{6,10},{7,11},{8,4},{9,5},... | collective-permute-start | bytes 786440 | tf_op jit(solution)/shard_map/ppermute | solution.py:21
  476.2 30.0 %collective-permute-start.112 = (f32[16,32,256]{2,1,0:T(8,128)S(1)}, f32[16,32,256]{2,1,0:T(8,128)S(1)}, u32[]{:S(2)}, u32[]{:S(2)}) collective-permute-start(f32[16,32,256]{2,1,0:T(8,128)S(1)} %get-tuple-element.163), channel_id=1, source_target_pairs={{0,16},{16,32},{32,48},{48,64},{64,80},{80,96},{96,112},{1,17},{17... | collective-permute-start | bytes 1572872 | tf_op jit(solution)/shard_map/ppermute | solution.py:35
  479.1 27.0 %collective-permute-start.107 = (bf16[16,32,256]{2,1,0:T(8,128)(2,1)S(1)}, bf16[16,32,256]{2,1,0:T(8,128)(2,1)S(1)}, u32[]{:S(2)}, u32[]{:S(2)}) collective-permute-start(bf16[16,32,256]{2,1,0:T(8,128)(2,1)S(1)} %get-tuple-element.160), channel_id=1, source_target_pairs={{16,0},{32,16},{48,32},{64,48},{80,64},{96,80},{112,96},{17,1},{33... | collective-permute-start | bytes 786440 | tf_op jit(solution)/shard_map/ppermute | solution.py:35
  480.4 15.1 %collective-permute-start.111 = (bf16[2,4,32,256]{3,2,1,0:T(8,128)(2,1)S(1)}, bf16[2,4,32,256]{3,2,1,0:T(8,128)(2,1)S(1)}, u32[]{:S(2)}, u32[]{:S(2)}) collective-permute-start(bf16[2,4,32,256]{3,2,1,0:T(8,128)(2,1)S(1)} %get-tuple-element.204.c0), channel_id=1, source_target_pairs={{0,48},{16,32},{32,16},{48,0},{64,112},{80,96},{96,80},{112,64},{1... | collective-permute-start | bytes 393224 | tf_op jit(solution)/shard_map/ppermute | solution.py:21
  513.2 14.4 %collective-permute-start.119 = (f32[2,4,32,256]{3,2,1,0:T(8,128)S(1)}, f32[2,4,32,256]{3,2,1,0:T(8,128)S(1)}, u32[]{:S(2)}, u32[]{:S(2)}) collective-permute-start(f32[2,4,32,256]{3,2,1,0:T(8,128)S(1)} %get-tuple-element.172), channel_id=1, source_target_pairs={{0,32},{16,48},{32,0},{48,16},{64,96},{80,112},{96,64},{112,80},{1... | collective-permute-start | bytes 786440 | tf_op jit(solution)/shard_map/ppermute | solution.py:21
  515.2 14.9 %collective-permute-start.120 = (f32[2,4,32,256]{3,2,1,0:T(8,128)S(1)}, f32[2,4,32,256]{3,2,1,0:T(8,128)S(1)}, u32[]{:S(2)}, u32[]{:S(2)}) collective-permute-start(f32[2,4,32,256]{3,2,1,0:T(8,128)S(1)} %get-tuple-element.173), channel_id=1, source_target_pairs={{0,48},{16,32},{32,16},{48,0},{64,112},{80,96},{96,80},{112,64},{1... | collective-permute-start | bytes 786440 | tf_op jit(solution)/shard_map/ppermute | solution.py:21
  516.2 17.8 %collective-permute-start.114 = (f32[2,4,32,256]{3,2,1,0:T(8,128)S(1)}, f32[2,4,32,256]{3,2,1,0:T(8,128)S(1)}, u32[]{:S(2)}, u32[]{:S(2)}) collective-permute-start(f32[2,4,32,256]{3,2,1,0:T(8,128)S(1)} %get-tuple-element.167), channel_id=1, source_target_pairs={{0,4},{1,5},{2,6},{3,7},{4,0},{5,1},{6,2},{7,3},{8,12},{9,13},{10,... | collective-permute-start | bytes 786440 | tf_op jit(solution)/shard_map/ppermute | solution.py:21
  517.0 17.0 %collective-permute-start.115 = (f32[2,4,32,256]{3,2,1,0:T(8,128)S(1)}, f32[2,4,32,256]{3,2,1,0:T(8,128)S(1)}, u32[]{:S(2)}, u32[]{:S(2)}) collective-permute-start(f32[2,4,32,256]{3,2,1,0:T(8,128)S(1)} %get-tuple-element.168), channel_id=1, source_target_pairs={{0,8},{1,9},{2,10},{3,11},{4,12},{5,13},{6,14},{7,15},{8,0},{9,1},... | collective-permute-start | bytes 786440 | tf_op jit(solution)/shard_map/ppermute | solution.py:21
  520.5 14.2 %collective-permute-start.116 = (f32[2,4,32,256]{3,2,1,0:T(8,128)S(1)}, f32[2,4,32,256]{3,2,1,0:T(8,128)S(1)}, u32[]{:S(2)}, u32[]{:S(2)}) collective-permute-start(f32[2,4,32,256]{3,2,1,0:T(8,128)S(1)} %get-tuple-element.169), channel_id=1, source_target_pairs={{0,12},{1,13},{2,14},{3,15},{4,8},{5,9},{6,10},{7,11},{8,4},{9,5},... | collective-permute-start | bytes 786440 | tf_op jit(solution)/shard_map/ppermute | solution.py:21
  (128 other events, 1202.6 us)

commit v2 on v1

v2 whole, which is shorter than its diff:
```python
import functools

import jax
import jax.numpy as jnp
from jax import lax
from jax.experimental import pallas as pl
from jax.experimental.pallas import tpu as pltpu
from jax.sharding import PartitionSpec as P

STEPS = 3
PRECISE = lax.Precision.HIGHEST
EPSILON = 1e-06
F32 = jnp.float32
BF16 = jnp.bfloat16
GROUP = 16
VMEM_BYTES = 40 * 1024 * 1024


def flip(value, axis, by):
    length = lax.axis_size(axis)
    return lax.ppermute(value, axis, [(i, i ^ by) for i in range(length)])


def flip_both(value, row_by, col_by):
    rows, cols = lax.axis_size("brow"), lax.axis_size("bcol")
    pairs = [
        (r * cols + c, (r ^ row_by) * cols + (c ^ col_by)) for r in range(rows) for c in range(cols)
    ]
    return lax.ppermute(value, ("brow", "bcol"), pairs)


def shifted(value, axis, by):
    length = lax.axis_size(axis)
    pairs = [(i, i + by) for i in range(length) if 0 <= i + by < length]
    return lax.ppermute(value, axis, pairs)


def sum_all(value):
    value = value + flip(value, "bcol", 1)
    value = (value + flip(value, "bcol", 4)) + (flip(value, "bcol", 8) + flip(value, "bcol", 12))
    value = (value + flip(value, "brow", 1)) + (flip(value, "brow", 2) + flip(value, "brow", 3))
    value = (value + flip(value, "bcol", 2)) + (flip(value, "brow", 4) + flip_both(value, 4, 2))
    return value


def whole(shape):
    return pl.BlockSpec(shape, lambda *_: (0,) * len(shape))


def params():
    return pltpu.CompilerParams(vmem_limit_bytes=VMEM_BYTES)


def assemble_kernel(ids, p0, p1, p2, p3, q0, q1, q2, q3, c0, c1, c2, c3, rows_out, rim_out, cols_out):
    mine, me = ids[0], ids[1]
    near, across, along = (p0, p1, p2, p3), (q0, q1, q2, q3), (c0, c1, c2, c3)
    for k in range(4):
        for half in range(2):
            for parity, refs in ((0, near), (1, across)):
                slab = me ^ (4 * k + 2 * half + parity)
                rows_out[pl.ds(4 * slab, 4)] = refs[k][half]
            slab = mine ^ (4 * half + k)
            cols_out[pl.ds(4 * slab, 4)] = along[k][half]
    rim_out[...] = rows_out[:16]


def assemble(ids, parts):
    return pl.pallas_call(
        assemble_kernel,
        grid_spec=pltpu.PrefetchScalarGridSpec(
            num_scalar_prefetch=1,
            grid=(1,),
            in_specs=[whole((2, 4, 32, 256))] * 12,
            out_specs=[whole((64, 32, 256)), whole((16, 32, 256)), whole((32, 32, 256))],
        ),
        out_shape=[
            jax.ShapeDtypeStruct((64, 32, 256), BF16),
            jax.ShapeDtypeStruct((16, 32, 256), BF16),
            jax.ShapeDtypeStruct((32, 32, 256), BF16),
        ],
        compiler_params=params(),
        cost_estimate=pl.CostEstimate(flops=0, bytes_accessed=3 << 20, transcendentals=0),
    )(ids, *parts)


def back_kernel(ids, band, rows, spread, spill):
    me = ids[1]
    step = pl.program_id(0)

    @pl.when(step == 0)
    def _():
        spread[:16] = jnp.zeros((16, 32, 256), F32)
        spread[64:] = jnp.zeros((16, 32, 256), F32)

    first = step * GROUP
    products = [
        jnp.dot(rows[first + g], band[g], preferred_element_type=F32) for g in range(GROUP)
    ]
    for g in range(GROUP):
        spread[first + g + me] = products[g]

    @pl.when(step == pl.num_programs(0) - 1)
    def _():
        spill[...] = spread[64:].astype(BF16)


def band_back(ids, band, rows):
    return pl.pallas_call(
        back_kernel,
        grid_spec=pltpu.PrefetchScalarGridSpec(
            num_scalar_prefetch=1,
            grid=(64 // GROUP,),
            in_specs=[
                pl.BlockSpec((GROUP, 256, 256), lambda i, *_: (i, 0, 0)),
                whole((64, 32, 256)),
            ],
            out_specs=[whole((80, 32, 256)), whole((16, 32, 256))],
        ),
        out_shape=[
            jax.ShapeDtypeStruct((80, 32, 256), F32),
            jax.ShapeDtypeStruct((16, 32, 256), BF16),
        ],
        compiler_params=params(),
        cost_estimate=pl.CostEstimate(
            flops=2 * 64 * 256 * 256 * 32, bytes_accessed=11 << 20, transcendentals=0
        ),
    )(ids, band, rows)


def far_kernel(ids, row_ids, col_ids, tiles, rows, cols, base, out, k0, k1, k2, k3, acc):
    mine, count = ids[0], ids[2]
    step = pl.program_id(0)

    @pl.when(step == 0)
    def _():
        out[...] = base[...]
        acc[...] = jnp.zeros_like(acc)

    def visit(base_slot, partial):
        first = step * GROUP + base_slot
        found = []
        for g in range(8):
            i = first + g
            live = i < count
            a, b = row_ids[i], col_ids[i]
            if partial:
                a, b = jnp.where(live, a, 0), jnp.where(live, b, 0)
            tile = tiles[base_slot + g]
            forward = lax.dot_general(
                cols[b], tile, (((1,), (1,)), ((), ())), preferred_element_type=F32
            )
            back = jnp.dot(rows[a], tile, preferred_element_type=F32)
            if partial:
                forward, back = jnp.where(live, forward, 0.0), jnp.where(live, back, 0.0)
            found.append((a, b, forward, back))
        for a, b, forward, back in found:
            out[a] += forward
            acc[b] += back

    for h in range(0, GROUP, 8):
        first = step * GROUP + h

        @pl.when(first + 8 <= count)
        def _():
            visit(h, False)

        @pl.when((first + 8 > count) & (first < count))
        def _():
            visit(h, True)

    @pl.when(step == pl.num_programs(0) - 1)
    def _():
        for j in range(8):
            piece = acc[pl.ds(4 * (mine ^ j), 4)]
            target = (k0, k1, k2, k3)[j & 3]
            target[j >> 2] = piece.astype(target.dtype)


PAIR = (2, 4, 32, 256)


def pair_shapes():
    return [jax.ShapeDtypeStruct(PAIR, F32)] + [jax.ShapeDtypeStruct(PAIR, BF16)] * 3


def far(ids, row_ids, col_ids, tiles, rows, cols, base):
    return pl.pallas_call(
        far_kernel,
        grid_spec=pltpu.PrefetchScalarGridSpec(
            num_scalar_prefetch=3,
            grid=(64 // GROUP,),
            in_specs=[
                pl.BlockSpec((GROUP, 256, 256), lambda i, *_: (i, 0, 0)),
                whole((64, 32, 256)),
                whole((32, 32, 256)),
                whole((64, 32, 256)),
            ],
            out_specs=[whole((64, 32, 256))] + [whole(PAIR)] * 4,
            scratch_shapes=[pltpu.VMEM((32, 32, 256), F32)],
        ),
        out_shape=[jax.ShapeDtypeStruct((64, 32, 256), F32)] + pair_shapes(),
        compiler_params=params(),
        cost_estimate=pl.CostEstimate(
            flops=4 * 64 * 256 * 256 * 32, bytes_accessed=15 << 20, transcendentals=0
        ),
    )(ids, row_ids, col_ids, tiles, rows, cols, base)


def forward_kernel(ids, band, rows, rim, base, spilled, halves, extended):
    me = ids[1]
    step = pl.program_id(0)

    @pl.when(step == 0)
    def _():
        extended[:64] = rows[...]
        extended[64:80] = rim[...]

    first = step * GROUP
    products = [
        lax.dot_general(
            extended[first + g + me], band[g], (((1,), (1,)), ((), ())), preferred_element_type=F32
        )
        + base[first + g]
        for g in range(GROUP)
    ]
    for h in range(GROUP // 4):
        slot = me ^ (step * (GROUP // 4) + h)
        for t in range(4):
            halves[slot & 1, slot >> 1, t] = products[4 * h + t]

    @pl.when(step == 0)
    def _():
        for h in range(4):
            slot = me ^ h
            for t in range(4):
                halves[slot & 1, slot >> 1, t] += spilled[4 * h + t].astype(F32)


def forward_split(ids, band, rows, rim, base, spilled, same, other, extended, halves):
    forward_kernel(ids, band, rows, rim, base, spilled, halves, extended)

    @pl.when(pl.program_id(0) == pl.num_programs(0) - 1)
    def _():
        same[...] = halves[0]
        other[...] = halves[1]


def band_forward(ids, band, rows, rim, base, spilled):
    return pl.pallas_call(
        forward_split,
        grid_spec=pltpu.PrefetchScalarGridSpec(
            num_scalar_prefetch=1,
            grid=(64 // GROUP,),
            in_specs=[
                pl.BlockSpec((GROUP, 256, 256), lambda i, *_: (i, 0, 0)),
                whole((64, 32, 256)),
                whole((16, 32, 256)),
                whole((64, 32, 256)),
                whole((16, 32, 256)),
            ],
            out_specs=[whole((8, 4, 32, 256))] * 2,
            scratch_shapes=[
                pltpu.VMEM((80, 32, 256), BF16),
                pltpu.VMEM((2, 8, 4, 32, 256), F32),
            ],
        ),
        out_shape=[jax.ShapeDtypeStruct((8, 4, 32, 256), F32)] * 2,
        compiler_params=params(),
        cost_estimate=pl.CostEstimate(
            flops=2 * 64 * 256 * 256 * 32, bytes_accessed=14 << 20, transcendentals=0
        ),
    )(ids, band, rows, rim, base, spilled)


def fold_kernel(same, arrived, *outs):
    for k in range(4):
        total = same[2 * k : 2 * k + 2] + arrived[2 * k : 2 * k + 2]
        outs[k][...] = total.astype(outs[k].dtype)


def fold(same, arrived):
    return pl.pallas_call(
        fold_kernel,
        out_shape=pair_shapes(),
        compiler_params=params(),
        cost_estimate=pl.CostEstimate(flops=0, bytes_accessed=3 << 20, transcendentals=0),
    )(same, arrived)


def against(left, right):
    return lax.dot_general(
        left, right, (((1,), (1,)), ((), ())), precision=PRECISE, preferred_element_type=F32
    )


def gram_kernel(n, with_images, *refs):
    basis, images = refs[: n + 1], refs[n + 1 : 2 * n + 1]
    terms = refs[2 * n + 1 : 2 * n + 5]
    mask, image_out, gram_out = refs[2 * n + 5 :]
    plain = jnp.zeros((32, 32 * (n + 1)), F32)
    cross = jnp.zeros((32, 32 * (n + 1)), F32)
    for t in range(4):
        image = ((terms[0][t] + terms[1][t]) + (terms[2][t] + terms[3][t])) * mask[t]
        image_out[t] = image
        newest = basis[-1][t]
        columns = jnp.concatenate([b[t] for b in basis], axis=0)
        plain += against(newest, columns)
        seen = jnp.concatenate([b[t] for b in images] + [image], axis=0)
        cross += 0.5 * (against(newest, seen) + against(image, columns))
    gram_out[...] = jnp.concatenate([plain, cross], axis=1)


def grams(older, older_images, newest, terms, mask):
    n = len(older)
    return pl.pallas_call(
        functools.partial(gram_kernel, n, True),
        out_shape=[
            jax.ShapeDtypeStruct((4, 32, 256), F32),
            jax.ShapeDtypeStruct((32, 64 * (n + 1)), F32),
        ],
        compiler_params=params(),
        cost_estimate=pl.CostEstimate(flops=1 << 27, bytes_accessed=1 << 20, transcendentals=0),
    )(*older, newest, *older_images, *terms, mask)


def mul(left, right):
    return jnp.dot(left, right, precision=PRECISE, preferred_element_type=F32)


def mul_left(left, right):
    return lax.dot_general(
        left, right, (((0,), (0,)), ((), ())), precision=PRECISE, preferred_element_type=F32
    )


def symmetric(matrix):
    return 0.5 * (matrix + matrix.T)


def unit(order):
    return (
        lax.broadcasted_iota(jnp.int32, (order, order), 0)
        == lax.broadcasted_iota(jnp.int32, (order, order), 1)
    ).astype(F32)


def block_inverse(matrix):
    order = matrix.shape[0]
    table = jnp.concatenate([matrix, unit(order)], axis=1)
    places = lax.broadcasted_iota(jnp.int32, (order, 1), 0)
    for k in range(order - 1):
        pivot = table[k : k + 1] / table[k : k + 1, k : k + 1]
        table = table - jnp.where(places > k, table[:, k : k + 1], 0.0) * pivot
    pivots = jnp.sum(table[:, :order] * unit(order), axis=1, keepdims=True)
    return table[:, order:] * lax.rsqrt(pivots)


def factor_inverse(matrix):
    order = matrix.shape[0]
    if order == 32:
        return block_inverse(matrix)
    head = block_inverse(matrix[:32, :32])
    edge = mul(head, matrix[:32, 32:])
    rest = factor_inverse(matrix[32:, 32:] - mul_left(edge, edge))
    lower = -mul(rest, mul_left(edge, head))
    return jnp.concatenate(
        [
            jnp.concatenate([head, jnp.zeros((32, order - 32), F32)], axis=1),
            jnp.concatenate([lower, rest], axis=1),
        ],
        axis=0,
    )


def joined(top, edge, corner):
    return jnp.concatenate(
        [jnp.concatenate([top, edge.T], axis=1), jnp.concatenate([edge, corner], axis=1)], axis=0
    )


def small_start(gram):
    inverse = block_inverse(symmetric(gram[:, :32]))
    return inverse, symmetric(against(mul(inverse, symmetric(gram[:, 32:])), inverse))


def small_step(known, known_images, gram):
    order = gram.shape[1] // 2
    edge = order - 32
    basis_gram = joined(known, gram[:, :edge], symmetric(gram[:, edge:order]))
    image_gram = joined(known_images, gram[:, order : order + edge], symmetric(gram[:, order + edge :]))
    head = lax.broadcasted_iota(jnp.int32, (1, order), 1) < 32
    down = lax.broadcasted_iota(jnp.int32, (order, 1), 0) < 32
    diagonal = basis_gram * unit(order)
    scale = jnp.where(head, 1.0, lax.rsqrt(jnp.sum(diagonal, axis=0, keepdims=True) + EPSILON))
    scale_down = jnp.where(down, 1.0, lax.rsqrt(jnp.sum(diagonal, axis=1, keepdims=True) + EPSILON))
    basis_gram = scale_down * basis_gram * scale
    image_gram = scale_down * image_gram * scale
    cross = basis_gram[32:, :32]
    tail = factor_inverse(basis_gram[32:, 32:] - against(cross, cross))
    inverse = jnp.concatenate(
        [
            jnp.concatenate([unit(32), jnp.zeros((32, edge), F32)], axis=1),
            jnp.concatenate([-mul(tail, cross), tail], axis=1),
        ],
        axis=0,
    )
    reduced = symmetric(against(mul(inverse, image_gram), inverse))
    size = jnp.sqrt(jnp.sum(jnp.sum(reduced * reduced, axis=1, keepdims=True), axis=0, keepdims=True))
    filtered = (reduced + size * unit(order)) / (2.0 * size)
    filtered = mul(filtered, filtered)
    leading = mul(filtered, filtered[:, :32])
    turned = mul(block_inverse(mul_left(leading, leading)), leading.T)
    weights = mul(turned, inverse)
    weights = jnp.concatenate([weights, jnp.where(head, 0.0, weights)], axis=0)
    next_basis = symmetric(against(mul(weights, basis_gram), weights))
    next_images = symmetric(against(mul(weights, image_gram), weights))
    return weights * scale, next_basis, next_images


def step_kernel(n, last, *refs):
    basis, images, mask, gram = refs[:n], refs[n : 2 * n], refs[2 * n], refs[2 * n + 1]
    if n == 1:
        outs = refs[2 * n + 2 :]
        weights, ritz = small_start(gram[...])
        next_basis, next_images = unit(32), ritz
    else:
        outs = refs[2 * n + 4 :]
        weights, next_basis, next_images = small_step(
            refs[2 * n + 2][...], refs[2 * n + 3][...], gram[...]
        )
        ritz = next_images[:32, :32]
    if last:
        outs[0][...] = ritz
        for t in range(4):
            outs[1][t] = mul(weights[:32], jnp.concatenate([b[t] for b in basis], axis=0))
        return
    outs[0][...] = next_basis
    outs[1][...] = next_images
    for t in range(4):
        moved = mul(weights, jnp.concatenate([b[t] for b in basis], axis=0))
        moved_images = mul(weights, jnp.concatenate([b[t] for b in images], axis=0))
        residual = moved_images[:32] - mul(ritz, moved[:32])
        outs[2][t] = (residual * mask[t]).astype(BF16)
        outs[3][t] = residual
        outs[4][t] = moved[:32]
        outs[5][t] = moved_images[:32]
        if n > 1:
            outs[6][t] = moved[32:]
            outs[7][t] = moved_images[32:]


def advance(basis, images, mask, gram, known, last=False):
    n = len(basis)
    slab = jax.ShapeDtypeStruct((4, 32, 256), F32)
    if last:
        outs = [jax.ShapeDtypeStruct((32, 32), F32), slab]
    else:
        order = 32 if n == 1 else 64
        outs = [jax.ShapeDtypeStruct((order, order), F32)] * 2
        outs += [jax.ShapeDtypeStruct((4, 32, 256), BF16)] + [slab] * (3 if n == 1 else 5)
    return pl.pallas_call(
        functools.partial(step_kernel, n, last),
        out_shape=outs,
        compiler_params=params(),
        cost_estimate=pl.CostEstimate(flops=1 << 28, bytes_accessed=1 << 20, transcendentals=0),
    )(*basis, *images, mask, gram, *known)


def body(x_start, bin_mask, band, off_tiles, off_rows, off_cols, off_count):
    width = x_start.shape[1]
    band = band[:, 0]
    tiles = off_tiles[0, 0]
    row_ids, col_ids = off_rows[0, 0], off_cols[0, 0]
    ids = jnp.stack(
        [lax.axis_index("brow"), lax.axis_index("bcol"), off_count[0, 0], jnp.int32(0)]
    ).astype(jnp.int32)
    mask = bin_mask.astype(F32).reshape(4, 1, 256)
    started = x_start.T.reshape(width, 4, 256).transpose(1, 0, 2) * mask

    def apply_operator(packed):
        pair = jnp.stack([packed, flip(packed, "bcol", 2)])
        near = [pair] + [flip(pair, "bcol", 4 * k) for k in (1, 2, 3)]
        across = [flip(part, "bcol", 1) for part in near]
        col_pair = jnp.stack([packed, flip(packed, "brow", 4)])
        along = [col_pair] + [flip(col_pair, "brow", k) for k in (1, 2, 3)]
        rows, rim, cols = assemble(ids, near + across + along)
        rim = shifted(rim, "brow", -1)
        spread, spill = band_back(ids, band, rows)
        spilled = shifted(spill, "brow", 1)
        base, *col_sums = far(ids, row_ids, col_ids, tiles, rows, cols, spread)
        c0, c1, c2, c3 = [col_sums[0]] + [
            flip(col_sums[k], "brow", k).astype(F32) for k in (1, 2, 3)
        ]
        col_total = (c0 + c1) + (c2 + c3)
        col_other = flip(col_total[1], "brow", 4)
        same, other = band_forward(ids, band, rows, rim, base, spilled)
        folded = fold(same, flip(other, "bcol", 1))
        r0, r1, r2, r3 = [folded[0]] + [
            flip(folded[k], "bcol", 4 * k).astype(F32) for k in (1, 2, 3)
        ]
        row_total = (r0 + r1) + (r2 + r3)
        row_other = flip(row_total[1], "bcol", 2)
        return [row_total[0], row_other, col_total[0], col_other]

    terms = apply_operator((started * mask).astype(BF16))
    image, gram = grams([], [], started, terms, mask)
    known_basis, known_images, packed, residual, vectors, images = advance(
        [started], [image], mask, sum_all(gram), []
    )
    older, older_images = [vectors], [images]
    for step in range(STEPS):
        terms = apply_operator(packed)
        residual_image, gram = grams(older, older_images, residual, terms, mask)
        outs = advance(
            older + [residual],
            older_images + [residual_image],
            mask,
            sum_all(gram),
            [known_basis, known_images],
            last=step == STEPS - 1,
        )
        if step < STEPS - 1:
            known_basis, known_images, packed, residual, vectors, images, tail, tail_images = outs
            older, older_images = [vectors, tail], [images, tail_images]
    ritz, vectors = outs
    return vectors.transpose(1, 0, 2).reshape(width, -1).T, ritz


def solution(mesh):
    return jax.shard_map(
        body,
        mesh=mesh,
        in_specs=(
            P(("brow", "bcol"), None),
            P(("brow", "bcol")),
            P("brow", "bcol", None, None),
            P("brow", "bcol", None, None, None),
            P("brow", "bcol", None),
            P("brow", "bcol", None),
            P("brow", "bcol"),
        ),
        out_specs=(P(("brow", "bcol"), None), P()),
        check_vma=False,
    )
```

time: 612 us -> 445 us (0.73)
  other arithmetic: 80.5 us -> 3.38 us
  waiting for transfers between devices: 197 us -> 152 us
  local copies, waits for them, and re-layouts: 22.5 us -> 4.23 us
  Pallas kernels: 112 us -> 100 us
  matrix products: 7.77 us -> 0 us
    another operation x35 -> x0, other arithmetic: 73.8 us -> none  [the longest x9 25.4 us: rayleigh_ritz(): factor = jnp.linalg.cholesky(basis_gram)]
    ppermute x120, waiting for transfers between devices: 191 us -> 149 us  [flip(): return lax.ppermute(value, axis, [(i, i ^ by) for i in range(length)])]
    pallas_call x4, Pallas kernels: 42.4 us -> 10.2 us  [band_back(): pl.pallas_call(back_kernel, grid_spec=pltpu.PrefetchScalarGridSpec(num_sc...]
    pallas_call x12, Pallas kernels: 23.5 us -> 53 us  [the longest x4 37.6 us: advance(): pl.pallas_call(functools.partial(step_kernel, n, last), out_shape=outs, c...]
    unnamed x56 -> x12, local copies, waits for them, and re-layouts: 14.8 us -> 3.4 us
    ppermute x120, starting transfers between devices: 145 us -> 135 us  [flip(): return lax.ppermute(value, axis, [(i, i ^ by) for i in range(length)])]
    pallas_call x4, Pallas kernels: 37.6 us -> 30.7 us  [far(): pl.pallas_call(far_kernel, grid_spec=pltpu.PrefetchScalarGridSpec(num_sca...]
  transfers between devices with their start and end apart: 132 -> 132, of which waited for: 88 -> 84; matrix products, arithmetic and copies ran while one was open for 1% -> 0% of each run, Pallas kernels for 6% -> 9%
where the time goes in v2:
time: 445 us; the launch traced here: 436 us
  starting transfers between devices  174 us (39%)
  waiting for transfers between devices  152 us (34%)
  Pallas kernels  100 us (22%)
    ppermute x120, waiting for transfers between devices, flip(): return lax.ppermute(value, axis, [(i, i ^ by) for i in range(length)])  149 us
    ppermute x120, starting transfers between devices, flip(): return lax.ppermute(value, axis, [(i, i ^ by) for i in range(length)])  135 us
    pallas_call x4, Pallas kernels, advance(): pl.pallas_call(functools.partial(step_kernel, n, last), out_shape=outs, c...  37.6 us
    pallas_call x4, Pallas kernels, far(): pl.pallas_call(far_kernel, grid_spec=pltpu.PrefetchScalarGridSpec(num_sca...  30.7 us
    ppermute x8, starting transfers between devices, shifted(): return lax.ppermute(value, axis, pairs)  23.7 us
    pallas_call x4, Pallas kernels, band_forward(): pl.pallas_call(forward_split, grid_spec=pltpu.PrefetchScalarGridSpec(num_...  15 us
    ppermute x4, starting transfers between devices, flip_both(): return lax.ppermute(value, ('brow', 'bcol'), pairs)  14.6 us
    pallas_call x4, Pallas kernels, band_back(): pl.pallas_call(back_kernel, grid_spec=pltpu.PrefetchScalarGridSpec(num_sc...  10.2 us
  transfers between devices with their start and end apart: 132, of which 84 were waited for; matrix products, arithmetic and copies ran while one was open for 0% of the time, Pallas kernels for 9%

profile of v2, /device:TPU:0, one launch (start us, length us, event | category | flops | bytes accessed | tf_op | source)
XLA Modules:
  0.0 436.3 jit_solution(15270897468233837722)
XLA Ops:
  9.9 4.1 collective-permute-start.11
  32.9 4.6 %collective-permute-start.13 = (bf16[16,32,256]{2,1,0:T(8,128)(2,1)S(1)}, bf16[16,32,256]{2,1,0:T(8,128)(2,1)S(1)}, u32[]{:S(2)}, u32[]{:S(2)}) collective-permute-start(bf16[16,32,256]{2,1,0:T(8,128)(2,1)S(1)} %get-tuple-element.103), channel_id=1, source_target_pairs={{0,16},{16,32},{32,48},{48,64},{64,80},{80,96},{96,112},{1,17},{17... | collective-permute-start | bytes 786440 | tf_op jit(solution)/shard_map/ppermute | solution.py:35
  37.5 7.9 %shard_map.88 = (f32[64,32,256]{2,1,0:T(8,128)S(1)}, f32[2,4,32,256]{3,2,1,0:T(8,128)S(1)}, bf16[2,4,32,256]{3,2,1,0:T(8,128)(2,1)S(1)}, bf16[2,4,32,256]{3,2,1,0:T(8,128)(2,1)S(1)}, bf16[2,4,32,256]{3,2,1,0:T(8,128)(2,1)S(1)}) custom-call(s32[4]{0:T(128)S(1)} %pad_add_fusion.ids, s32[64]{0:T(128)S(1)} %bitcast.97, s32[64]{0:T(128)S(1)} %bitcast.101, ...), custom_call_target="tpu_custom_call" | custom-call | flops 536870912 | bytes 15728640 | tf_op jit(solution)/shard_map/pallas_call | solution.py:187
  50.9 6.1 %collective-permute-start.20 = (bf16[2,4,32,256]{3,2,1,0:T(8,128)(2,1)S(1)}, bf16[2,4,32,256]{3,2,1,0:T(8,128)(2,1)S(1)}, u32[]{:S(2)}, u32[]{:S(2)}) collective-permute-start(bf16[2,4,32,256]{3,2,1,0:T(8,128)(2,1)S(1)} %get-tuple-element.112), channel_id=1, source_target_pairs={{0,32},{16,48},{32,0},{48,16},{64,96},{80,112},{96,64},{112,80},{1... | collective-permute-start | bytes 393224 | tf_op jit(solution)/shard_map/ppermute | solution.py:21
  57.0 6.7 %collective-permute-done.20 = bf16[2,4,32,256]{3,2,1,0:T(8,128)(2,1)S(1)} collective-permute-done((bf16[2,4,32,256]{3,2,1,0:T(8,128)(2,1)S(1)}, bf16[2,4,32,256]{3,2,1,0:T(8,128)(2,1)S(1)}, u32[]{:S(2)}, u32[]{:S(2)}) %collective-permute-start.20) | collective-permute-done | bytes 131104 | tf_op jit(solution)/shard_map/ppermute | solution.py:21
  78.2 4.8 %collective-permute-done.18.refs_2_ = f32[4,32,256]{2,1,0:T(8,128)S(1)} collective-permute-done((f32[4,32,256]{2,1,0:T(8,128)S(1)}, f32[4,32,256]{2,1,0:T(8,128)S(1)}, u32[]{:S(2)}, u32[]{:S(2)}) %collective-permute-start.18) | collective-permute-done | bytes 131104 | tf_op jit(solution)/shard_map/ppermute | solution.py:21
  91.6 3.9 collective-permute-start.27
  133.5 4.6 %collective-permute-start.46 = (bf16[16,32,256]{2,1,0:T(8,128)(2,1)S(1)}, bf16[16,32,256]{2,1,0:T(8,128)(2,1)S(1)}, u32[]{:S(2)}, u32[]{:S(2)}) collective-permute-start(bf16[16,32,256]{2,1,0:T(8,128)(2,1)S(1)} %get-tuple-element.125), channel_id=1, source_target_pairs={{0,16},{16,32},{32,48},{48,64},{64,80},{80,96},{96,112},{1,17},{17... | collective-permute-start | bytes 786440 | tf_op jit(solution)/shard_map/ppermute | solution.py:35
  138.1 7.6 %shard_map.95 = (f32[64,32,256]{2,1,0:T(8,128)S(1)}, f32[2,4,32,256]{3,2,1,0:T(8,128)S(1)}, bf16[2,4,32,256]{3,2,1,0:T(8,128)(2,1)S(1)}, bf16[2,4,32,256]{3,2,1,0:T(8,128)(2,1)S(1)}, bf16[2,4,32,256]{3,2,1,0:T(8,128)(2,1)S(1)}) custom-call(s32[4]{0:T(128)S(1)} %pad_add_fusion.ids, s32[64]{0:T(128)S(1)} %bitcast.98, s32[64]{0:T(128)S(1)} %bitcast.102, ...), custom_call_target="tpu_custom_call" | custom-call | flops 536870912 | bytes 15728640 | tf_op jit(solution)/shard_map/pallas_call | solution.py:187
  145.7 3.8 shard_map.96
  151.0 5.6 %collective-permute-start.53 = (bf16[2,4,32,256]{3,2,1,0:T(8,128)(2,1)S(1)}, bf16[2,4,32,256]{3,2,1,0:T(8,128)(2,1)S(1)}, u32[]{:S(2)}, u32[]{:S(2)}) collective-permute-start(bf16[2,4,32,256]{3,2,1,0:T(8,128)(2,1)S(1)} %get-tuple-element.134), channel_id=1, source_target_pairs={{0,32},{16,48},{32,0},{48,16},{64,96},{80,112},{96,64},{112,80},{1... | collective-permute-start | bytes 393224 | tf_op jit(solution)/shard_map/ppermute | solution.py:21
  156.6 6.7 %collective-permute-done.53 = bf16[2,4,32,256]{3,2,1,0:T(8,128)(2,1)S(1)} collective-permute-done((bf16[2,4,32,256]{3,2,1,0:T(8,128)(2,1)S(1)}, bf16[2,4,32,256]{3,2,1,0:T(8,128)(2,1)S(1)}, u32[]{:S(2)}, u32[]{:S(2)}) %collective-permute-start.53) | collective-permute-done | bytes 131104 | tf_op jit(solution)/shard_map/ppermute | solution.py:21
  177.4 4.2 collective-permute-done.51.refs_4_
  191.5 4.0 collective-permute-start.60
  197.3 3.8 collective-permute-start.65
  206.4 9.0 %shard_map.99 = (f32[64,64]{1,0:T(8,128)S(1)}, f32[64,64]{1,0:T(8,128)S(1)}, bf16[4,32,256]{2,1,0:T(8,128)(2,1)S(1)}, f32[4,32,256]{2,1,0:T(8,128)S(1)}, f32[4,3...) custom-call(f32[4,32,256]{2,1,0:T(8,128)S(1)} %get-tuple-element.116.refs, ...), custom_call_target="tpu_custom_call" | custom-call | flops 268435456 | bytes 1048576 | tf_op jit(solution)/shard_map/pallas_call | solution.py:461
  239.0 4.6 %collective-permute-start.79 = (bf16[16,32,256]{2,1,0:T(8,128)(2,1)S(1)}, bf16[16,32,256]{2,1,0:T(8,128)(2,1)S(1)}, u32[]{:S(2)}, u32[]{:S(2)}) collective-permute-start(bf16[16,32,256]{2,1,0:T(8,128)(2,1)S(1)} %get-tuple-element.151), channel_id=1, source_target_pairs={{0,16},{16,32},{32,48},{48,64},{64,80},{80,96},{96,112},{1,17},{17... | collective-permute-start | bytes 786440 | tf_op jit(solution)/shard_map/ppermute | solution.py:35
  243.6 7.6 %shard_map.102 = (f32[64,32,256]{2,1,0:T(8,128)S(1)}, f32[2,4,32,256]{3,2,1,0:T(8,128)S(1)}, bf16[2,4,32,256]{3,2,1,0:T(8,128)(2,1)S(1)}, bf16[2,4,32,256]{3,2,1,0:T(8,128)(2,1)S(1)}, bf16[2,4,32,256]{3,2,1,0:T(8,128)(2,1)S(1)}) custom-call(s32[4]{0:T(128)S(1)} %pad_add_fusion.ids, s32[64]{0:T(128)S(1)} %bitcast.99, s32[64]{0:T(128)S(1)} %bitcast.103, ...), custom_call_target="tpu_custom_call" | custom-call | flops 536870912 | bytes 15728640 | tf_op jit(solution)/shard_map/pallas_call | solution.py:187
  251.3 3.8 shard_map.103
  256.5 5.6 %collective-permute-start.86 = (bf16[2,4,32,256]{3,2,1,0:T(8,128)(2,1)S(1)}, bf16[2,4,32,256]{3,2,1,0:T(8,128)(2,1)S(1)}, u32[]{:S(2)}, u32[]{:S(2)}) collective-permute-start(bf16[2,4,32,256]{3,2,1,0:T(8,128)(2,1)S(1)} %get-tuple-element.160), channel_id=1, source_target_pairs={{0,32},{16,48},{32,0},{48,16},{64,96},{80,112},{96,64},{112,80},{1... | collective-permute-start | bytes 393224 | tf_op jit(solution)/shard_map/ppermute | solution.py:21
  262.3 6.5 %collective-permute-done.86 = bf16[2,4,32,256]{3,2,1,0:T(8,128)(2,1)S(1)} collective-permute-done((bf16[2,4,32,256]{3,2,1,0:T(8,128)(2,1)S(1)}, bf16[2,4,32,256]{3,2,1,0:T(8,128)(2,1)S(1)}, u32[]{:S(2)}, u32[]{:S(2)}) %collective-permute-start.86) | collective-permute-done | bytes 131104 | tf_op jit(solution)/shard_map/ppermute | solution.py:21
  283.1 4.3 collective-permute-done.84.refs_6_
  297.6 4.0 collective-permute-start.93
  312.9 12.6 %shard_map.106 = (f32[64,64]{1,0:T(8,128)S(1)}, f32[64,64]{1,0:T(8,128)S(1)}, bf16[4,32,256]{2,1,0:T(8,128)(2,1)S(1)}, f32[4,32,256]{2,1,0:T(8,128)S(1)}, f32[4,...) custom-call(f32[4,32,256]{2,1,0:T(8,128)S(1)} %get-tuple-element.140.ref, ...), custom_call_target="tpu_custom_call" | custom-call | flops 268435456 | bytes 1048576 | tf_op jit(solution)/shard_map/pallas_call | solution.py:461
  349.3 4.6 %collective-permute-start.112 = (bf16[16,32,256]{2,1,0:T(8,128)(2,1)S(1)}, bf16[16,32,256]{2,1,0:T(8,128)(2,1)S(1)}, u32[]{:S(2)}, u32[]{:S(2)}) collective-permute-start(bf16[16,32,256]{2,1,0:T(8,128)(2,1)S(1)} %get-tuple-element.177), channel_id=1, source_target_pairs={{0,16},{16,32},{32,48},{48,64},{64,80},{80,96},{96,112},{1,17},{17... | collective-permute-start | bytes 786440 | tf_op jit(solution)/shard_map/ppermute | solution.py:35
  353.9 7.6 %shard_map.109 = (f32[64,32,256]{2,1,0:T(8,128)S(1)}, f32[2,4,32,256]{3,2,1,0:T(8,128)S(1)}, bf16[2,4,32,256]{3,2,1,0:T(8,128)(2,1)S(1)}, bf16[2,4,32,256]{3,2,1,0:T(8,128)(2,1)S(1)}, bf16[2,4,32,256]{3,2,1,0:T(8,128)(2,1)S(1)}) custom-call(s32[4]{0:T(128)S(1)} %pad_add_fusion.ids, s32[64]{0:T(128)S(1)} %bitcast.100, s32[64]{0:T(128)S(1)} %bitcast.104, ...), custom_call_target="tpu_custom_call" | custom-call | flops 536870912 | bytes 15728640 | tf_op jit(solution)/shard_map/pallas_call | solution.py:187
  361.5 3.7 shard_map.110
  366.8 5.6 %collective-permute-start.119 = (bf16[2,4,32,256]{3,2,1,0:T(8,128)(2,1)S(1)}, bf16[2,4,32,256]{3,2,1,0:T(8,128)(2,1)S(1)}, u32[]{:S(2)}, u32[]{:S(2)}) collective-permute-start(bf16[2,4,32,256]{3,2,1,0:T(8,128)(2,1)S(1)} %get-tuple-element.186), channel_id=1, source_target_pairs={{0,32},{16,48},{32,0},{48,16},{64,96},{80,112},{96,64},{112,80},{1... | collective-permute-start | bytes 393224 | tf_op jit(solution)/shard_map/ppermute | solution.py:21
  372.4 6.7 %collective-permute-done.119 = bf16[2,4,32,256]{3,2,1,0:T(8,128)(2,1)S(1)} collective-permute-done((bf16[2,4,32,256]{3,2,1,0:T(8,128)(2,1)S(1)}, bf16[2,4,32,256]{3,2,1,0:T(8,128)(2,1)S(1)}, u32[]{:S(2)}, u32[]{:S(2)}) %collective-permute-start.119) | collective-permute-done | bytes 131104 | tf_op jit(solution)/shard_map/ppermute | solution.py:21
  393.2 4.2 collective-permute-done.117.refs_6_
  407.6 4.0 collective-permute-start.126
  422.9 12.3 %shard_map.113 = (f32[32,32]{1,0:T(8,128)}, f32[4,32,256]{2,1,0:T(8,128)S(1)}) custom-call(f32[4,32,256]{2,1,0:T(8,128)S(1)} %get-tuple-element.166.refs_0_, f32[4,32,256]{2,1,0:T(8,128)S(1)} %get-tuple-element.167.refs_1_, f32[4,32,256]{2,1,0:T(8,128)S(1)} %get-tuple-element.168.refs_2_, f32[4,32,256]{2,1,0:T(8,128)S(1)} %get-tuple-element.169.refs_3_, ...), custom_call_target="tpu_custom_call" | custom-call | flops 268435456 | bytes 1048576 | tf_op jit(solution)/shard_map/pallas_call | solution.py:461
  (316 shorter events, 248.7 us)
Async XLA Ops:
  9.9 8.5 %collective-permute-start.11 = (bf16[2,4,32,256]{3,2,1,0:T(8,128)(2,1)S(1)}, bf16[2,4,32,256]{3,2,1,0:T(8,128)(2,1)S(1)}, u32[]{:S(2)}, u32[]{:S(2)}) collective-permute-start(bf16[2,4,32,256]{3,2,1,0:T(8,128)(2,1)S(1)} %get-tuple-element.216.c0), channel_id=1, source_target_pairs={{0,48},{16,32},{32,16},{48,0},{64,112},{80,96},{96,80},{112,64},{1... | collective-permute-start | bytes 393224 | tf_op jit(solution)/shard_map/ppermute | solution.py:21
  25.7 19.7 %collective-permute-start.12 = (bf16[16,32,256]{2,1,0:T(8,128)(2,1)S(1)}, bf16[16,32,256]{2,1,0:T(8,128)(2,1)S(1)}, u32[]{:S(2)}, u32[]{:S(2)}) collective-permute-start(bf16[16,32,256]{2,1,0:T(8,128)(2,1)S(1)} %get-tuple-element.99), channel_id=1, source_target_pairs={{16,0},{32,16},{48,32},{64,48},{80,64},{96,80},{112,96},{17,1},{33... | collective-permute-start | bytes 786440 | tf_op jit(solution)/shard_map/ppermute | solution.py:35
  32.9 12.5 %collective-permute-start.13 = (bf16[16,32,256]{2,1,0:T(8,128)(2,1)S(1)}, bf16[16,32,256]{2,1,0:T(8,128)(2,1)S(1)}, u32[]{:S(2)}, u32[]{:S(2)}) collective-permute-start(bf16[16,32,256]{2,1,0:T(8,128)(2,1)S(1)} %get-tuple-element.103), channel_id=1, source_target_pairs={{0,16},{16,32},{32,48},{48,64},{64,80},{80,96},{96,112},{1,17},{17... | collective-permute-start | bytes 786440 | tf_op jit(solution)/shard_map/ppermute | solution.py:35
  49.2 16.9 %collective-permute-start.14 = (f32[8,4,32,256]{3,2,1,0:T(8,128)S(1)}, f32[8,4,32,256]{3,2,1,0:T(8,128)S(1)}, u32[]{:S(2)}, u32[]{:S(2)}) collective-permute-start(f32[8,4,32,256]{3,2,1,0:T(8,128)S(1)} %get-tuple-element.105), channel_id=1, source_target_pairs={{0,1},{1,0},{2,3},{3,2},{4,5},{5,4},{6,7},{7,6},{8,9},{9,8},{10,11... | collective-permute-start | bytes 3145736 | tf_op jit(solution)/shard_map/ppermute | solution.py:21
  50.9 12.8 %collective-permute-start.20 = (bf16[2,4,32,256]{3,2,1,0:T(8,128)(2,1)S(1)}, bf16[2,4,32,256]{3,2,1,0:T(8,128)(2,1)S(1)}, u32[]{:S(2)}, u32[]{:S(2)}) collective-permute-start(bf16[2,4,32,256]{3,2,1,0:T(8,128)(2,1)S(1)} %get-tuple-element.112), channel_id=1, source_target_pairs={{0,32},{16,48},{32,0},{48,16},{64,96},{80,112},{96,64},{112,80},{1... | collective-permute-start | bytes 393224 | tf_op jit(solution)/shard_map/ppermute | solution.py:21
  57.0 9.1 %collective-permute-start.21 = (bf16[2,4,32,256]{3,2,1,0:T(8,128)(2,1)S(1)}, bf16[2,4,32,256]{3,2,1,0:T(8,128)(2,1)S(1)}, u32[]{:S(2)}, u32[]{:S(2)}) collective-permute-start(bf16[2,4,32,256]{3,2,1,0:T(8,128)(2,1)S(1)} %get-tuple-element.113), channel_id=1, source_target_pairs={{0,48},{16,32},{32,16},{48,0},{64,112},{80,96},{96,80},{112,64},{1... | collective-permute-start | bytes 393224 | tf_op jit(solution)/shard_map/ppermute | solution.py:21
  67.0 8.9 %collective-permute-start.16 = (bf16[2,4,32,256]{3,2,1,0:T(8,128)(2,1)S(1)}, bf16[2,4,32,256]{3,2,1,0:T(8,128)(2,1)S(1)}, u32[]{:S(2)}, u32[]{:S(2)}) collective-permute-start(bf16[2,4,32,256]{3,2,1,0:T(8,128)(2,1)S(1)} %get-tuple-element.108), channel_id=1, source_target_pairs={{0,8},{1,9},{2,10},{3,11},{4,12},{5,13},{6,14},{7,15},{8,0},{9,1},... | collective-permute-start | bytes 393224 | tf_op jit(solution)/shard_map/ppermute | solution.py:21
  69.9 8.0 %collective-permute-start.17 = (bf16[2,4,32,256]{3,2,1,0:T(8,128)(2,1)S(1)}, bf16[2,4,32,256]{3,2,1,0:T(8,128)(2,1)S(1)}, u32[]{:S(2)}, u32[]{:S(2)}) collective-permute-start(bf16[2,4,32,256]{3,2,1,0:T(8,128)(2,1)S(1)} %get-tuple-element.109), channel_id=1, source_target_pairs={{0,12},{1,13},{2,14},{3,15},{4,8},{5,9},{6,10},{7,11},{8,4},{9,5},... | collective-permute-start | bytes 393224 | tf_op jit(solution)/shard_map/ppermute | solution.py:21
  116.3 7.7 %collective-permute-start.44 = (bf16[2,4,32,256]{3,2,1,0:T(8,128)(2,1)S(1)}, bf16[2,4,32,256]{3,2,1,0:T(8,128)(2,1)S(1)}, u32[]{:S(2)}, u32[]{:S(2)}) collective-permute-start(bf16[2,4,32,256]{3,2,1,0:T(8,128)(2,1)S(1)} %get-tuple-element.214.c0), channel_id=1, source_target_pairs={{0,48},{16,32},{32,16},{48,0},{64,112},{80,96},{96,80},{112,64},{1... | collective-permute-start | bytes 393224 | tf_op jit(solution)/shard_map/ppermute | solution.py:21
  129.7 16.1 %collective-permute-start.45 = (bf16[16,32,256]{2,1,0:T(8,128)(2,1)S(1)}, bf16[16,32,256]{2,1,0:T(8,128)(2,1)S(1)}, u32[]{:S(2)}, u32[]{:S(2)}) collective-permute-start(bf16[16,32,256]{2,1,0:T(8,128)(2,1)S(1)} %get-tuple-element.121), channel_id=1, source_target_pairs={{16,0},{32,16},{48,32},{64,48},{80,64},{96,80},{112,96},{17,1},{33... | collective-permute-start | bytes 786440 | tf_op jit(solution)/shard_map/ppermute | solution.py:35
  133.5 12.2 %collective-permute-start.46 = (bf16[16,32,256]{2,1,0:T(8,128)(2,1)S(1)}, bf16[16,32,256]{2,1,0:T(8,128)(2,1)S(1)}, u32[]{:S(2)}, u32[]{:S(2)}) collective-permute-start(bf16[16,32,256]{2,1,0:T(8,128)(2,1)S(1)} %get-tuple-element.125), channel_id=1, source_target_pairs={{0,16},{16,32},{32,48},{48,64},{64,80},{80,96},{96,112},{1,17},{17... | collective-permute-start | bytes 786440 | tf_op jit(solution)/shard_map/ppermute | solution.py:35
  149.5 16.3 %collective-permute-start.47 = (f32[8,4,32,256]{3,2,1,0:T(8,128)S(1)}, f32[8,4,32,256]{3,2,1,0:T(8,128)S(1)}, u32[]{:S(2)}, u32[]{:S(2)}) collective-permute-start(f32[8,4,32,256]{3,2,1,0:T(8,128)S(1)} %get-tuple-element.127), channel_id=1, source_target_pairs={{0,1},{1,0},{2,3},{3,2},{4,5},{5,4},{6,7},{7,6},{8,9},{9,8},{10,11... | collective-permute-start | bytes 3145736 | tf_op jit(solution)/shard_map/ppermute | solution.py:21
  151.0 12.4 %collective-permute-start.53 = (bf16[2,4,32,256]{3,2,1,0:T(8,128)(2,1)S(1)}, bf16[2,4,32,256]{3,2,1,0:T(8,128)(2,1)S(1)}, u32[]{:S(2)}, u32[]{:S(2)}) collective-permute-start(bf16[2,4,32,256]{3,2,1,0:T(8,128)(2,1)S(1)} %get-tuple-element.134), channel_id=1, source_target_pairs={{0,32},{16,48},{32,0},{48,16},{64,96},{80,112},{96,64},{112,80},{1... | collective-permute-start | bytes 393224 | tf_op jit(solution)/shard_map/ppermute | solution.py:21
  156.6 9.1 %collective-permute-start.54 = (bf16[2,4,32,256]{3,2,1,0:T(8,128)(2,1)S(1)}, bf16[2,4,32,256]{3,2,1,0:T(8,128)(2,1)S(1)}, u32[]{:S(2)}, u32[]{:S(2)}) collective-permute-start(bf16[2,4,32,256]{3,2,1,0:T(8,128)(2,1)S(1)} %get-tuple-element.135), channel_id=1, source_target_pairs={{0,48},{16,32},{32,16},{48,0},{64,112},{80,96},{96,80},{112,64},{1... | collective-permute-start | bytes 393224 | tf_op jit(solution)/shard_map/ppermute | solution.py:21
  166.4 8.1 %collective-permute-start.49 = (bf16[2,4,32,256]{3,2,1,0:T(8,128)(2,1)S(1)}, bf16[2,4,32,256]{3,2,1,0:T(8,128)(2,1)S(1)}, u32[]{:S(2)}, u32[]{:S(2)}) collective-permute-start(bf16[2,4,32,256]{3,2,1,0:T(8,128)(2,1)S(1)} %get-tuple-element.130), channel_id=1, source_target_pairs={{0,8},{1,9},{2,10},{3,11},{4,12},{5,13},{6,14},{7,15},{8,0},{9,1},... | collective-permute-start | bytes 393224 | tf_op jit(solution)/shard_map/ppermute | solution.py:21
  168.5 8.0 %collective-permute-start.50 = (bf16[2,4,32,256]{3,2,1,0:T(8,128)(2,1)S(1)}, bf16[2,4,32,256]{3,2,1,0:T(8,128)(2,1)S(1)}, u32[]{:S(2)}, u32[]{:S(2)}) collective-permute-start(bf16[2,4,32,256]{3,2,1,0:T(8,128)(2,1)S(1)} %get-tuple-element.131), channel_id=1, source_target_pairs={{0,12},{1,13},{2,14},{3,15},{4,8},{5,9},{6,10},{7,11},{8,4},{9,5},... | collective-permute-start | bytes 393224 | tf_op jit(solution)/shard_map/ppermute | solution.py:21
  221.8 7.7 %collective-permute-start.77 = (bf16[2,4,32,256]{3,2,1,0:T(8,128)(2,1)S(1)}, bf16[2,4,32,256]{3,2,1,0:T(8,128)(2,1)S(1)}, u32[]{:S(2)}, u32[]{:S(2)}) collective-permute-start(bf16[2,4,32,256]{3,2,1,0:T(8,128)(2,1)S(1)} %get-tuple-element.212.c0), channel_id=1, source_target_pairs={{0,48},{16,32},{32,16},{48,0},{64,112},{80,96},{96,80},{112,64},{1... | collective-permute-start | bytes 393224 | tf_op jit(solution)/shard_map/ppermute | solution.py:21
  235.2 16.1 %collective-permute-start.78 = (bf16[16,32,256]{2,1,0:T(8,128)(2,1)S(1)}, bf16[16,32,256]{2,1,0:T(8,128)(2,1)S(1)}, u32[]{:S(2)}, u32[]{:S(2)}) collective-permute-start(bf16[16,32,256]{2,1,0:T(8,128)(2,1)S(1)} %get-tuple-element.147), channel_id=1, source_target_pairs={{16,0},{32,16},{48,32},{64,48},{80,64},{96,80},{112,96},{17,1},{33... | collective-permute-start | bytes 786440 | tf_op jit(solution)/shard_map/ppermute | solution.py:35
  239.0 12.2 %collective-permute-start.79 = (bf16[16,32,256]{2,1,0:T(8,128)(2,1)S(1)}, bf16[16,32,256]{2,1,0:T(8,128)(2,1)S(1)}, u32[]{:S(2)}, u32[]{:S(2)}) collective-permute-start(bf16[16,32,256]{2,1,0:T(8,128)(2,1)S(1)} %get-tuple-element.151), channel_id=1, source_target_pairs={{0,16},{16,32},{32,48},{48,64},{64,80},{80,96},{96,112},{1,17},{17... | collective-permute-start | bytes 786440 | tf_op jit(solution)/shard_map/ppermute | solution.py:35
  255.0 16.4 %collective-permute-start.80 = (f32[8,4,32,256]{3,2,1,0:T(8,128)S(1)}, f32[8,4,32,256]{3,2,1,0:T(8,128)S(1)}, u32[]{:S(2)}, u32[]{:S(2)}) collective-permute-start(f32[8,4,32,256]{3,2,1,0:T(8,128)S(1)} %get-tuple-element.153), channel_id=1, source_target_pairs={{0,1},{1,0},{2,3},{3,2},{4,5},{5,4},{6,7},{7,6},{8,9},{9,8},{10,11... | collective-permute-start | bytes 3145736 | tf_op jit(solution)/shard_map/ppermute | solution.py:21
  256.5 12.3 %collective-permute-start.86 = (bf16[2,4,32,256]{3,2,1,0:T(8,128)(2,1)S(1)}, bf16[2,4,32,256]{3,2,1,0:T(8,128)(2,1)S(1)}, u32[]{:S(2)}, u32[]{:S(2)}) collective-permute-start(bf16[2,4,32,256]{3,2,1,0:T(8,128)(2,1)S(1)} %get-tuple-element.160), channel_id=1, source_target_pairs={{0,32},{16,48},{32,0},{48,16},{64,96},{80,112},{96,64},{112,80},{1... | collective-permute-start | bytes 393224 | tf_op jit(solution)/shard_map/ppermute | solution.py:21
  262.1 9.2 %collective-permute-start.87 = (bf16[2,4,32,256]{3,2,1,0:T(8,128)(2,1)S(1)}, bf16[2,4,32,256]{3,2,1,0:T(8,128)(2,1)S(1)}, u32[]{:S(2)}, u32[]{:S(2)}) collective-permute-start(bf16[2,4,32,256]{3,2,1,0:T(8,128)(2,1)S(1)} %get-tuple-element.161), channel_id=1, source_target_pairs={{0,48},{16,32},{32,16},{48,0},{64,112},{80,96},{96,80},{112,64},{1... | collective-permute-start | bytes 393224 | tf_op jit(solution)/shard_map/ppermute | solution.py:21
  272.0 8.2 %collective-permute-start.82 = (bf16[2,4,32,256]{3,2,1,0:T(8,128)(2,1)S(1)}, bf16[2,4,32,256]{3,2,1,0:T(8,128)(2,1)S(1)}, u32[]{:S(2)}, u32[]{:S(2)}) collective-permute-start(bf16[2,4,32,256]{3,2,1,0:T(8,128)(2,1)S(1)} %get-tuple-element.156), channel_id=1, source_target_pairs={{0,8},{1,9},{2,10},{3,11},{4,12},{5,13},{6,14},{7,15},{8,0},{9,1},... | collective-permute-start | bytes 393224 | tf_op jit(solution)/shard_map/ppermute | solution.py:21
  274.1 8.1 %collective-permute-start.83 = (bf16[2,4,32,256]{3,2,1,0:T(8,128)(2,1)S(1)}, bf16[2,4,32,256]{3,2,1,0:T(8,128)(2,1)S(1)}, u32[]{:S(2)}, u32[]{:S(2)}) collective-permute-start(bf16[2,4,32,256]{3,2,1,0:T(8,128)(2,1)S(1)} %get-tuple-element.157), channel_id=1, source_target_pairs={{0,12},{1,13},{2,14},{3,15},{4,8},{5,9},{6,10},{7,11},{8,4},{9,5},... | collective-permute-start | bytes 393224 | tf_op jit(solution)/shard_map/ppermute | solution.py:21
  331.9 7.7 %collective-permute-start.110 = (bf16[2,4,32,256]{3,2,1,0:T(8,128)(2,1)S(1)}, bf16[2,4,32,256]{3,2,1,0:T(8,128)(2,1)S(1)}, u32[]{:S(2)}, u32[]{:S(2)}) collective-permute-start(bf16[2,4,32,256]{3,2,1,0:T(8,128)(2,1)S(1)} %get-tuple-element.210.c0), channel_id=1, source_target_pairs={{0,48},{16,32},{32,16},{48,0},{64,112},{80,96},{96,80},{112,64},{1... | collective-permute-start | bytes 393224 | tf_op jit(solution)/shard_map/ppermute | solution.py:21
  345.2 16.3 %collective-permute-start.111 = (bf16[16,32,256]{2,1,0:T(8,128)(2,1)S(1)}, bf16[16,32,256]{2,1,0:T(8,128)(2,1)S(1)}, u32[]{:S(2)}, u32[]{:S(2)}) collective-permute-start(bf16[16,32,256]{2,1,0:T(8,128)(2,1)S(1)} %get-tuple-element.173), channel_id=1, source_target_pairs={{16,0},{32,16},{48,32},{64,48},{80,64},{96,80},{112,96},{17,1},{33... | collective-permute-start | bytes 786440 | tf_op jit(solution)/shard_map/ppermute | solution.py:35
  349.3 12.2 %collective-permute-start.112 = (bf16[16,32,256]{2,1,0:T(8,128)(2,1)S(1)}, bf16[16,32,256]{2,1,0:T(8,128)(2,1)S(1)}, u32[]{:S(2)}, u32[]{:S(2)}) collective-permute-start(bf16[16,32,256]{2,1,0:T(8,128)(2,1)S(1)} %get-tuple-element.177), channel_id=1, source_target_pairs={{0,16},{16,32},{32,48},{48,64},{64,80},{80,96},{96,112},{1,17},{17... | collective-permute-start | bytes 786440 | tf_op jit(solution)/shard_map/ppermute | solution.py:35
  365.3 16.3 %collective-permute-start.113 = (f32[8,4,32,256]{3,2,1,0:T(8,128)S(1)}, f32[8,4,32,256]{3,2,1,0:T(8,128)S(1)}, u32[]{:S(2)}, u32[]{:S(2)}) collective-permute-start(f32[8,4,32,256]{3,2,1,0:T(8,128)S(1)} %get-tuple-element.179), channel_id=1, source_target_pairs={{0,1},{1,0},{2,3},{3,2},{4,5},{5,4},{6,7},{7,6},{8,9},{9,8},{10,11... | collective-permute-start | bytes 3145736 | tf_op jit(solution)/shard_map/ppermute | solution.py:21
  366.8 12.4 %collective-permute-start.119 = (bf16[2,4,32,256]{3,2,1,0:T(8,128)(2,1)S(1)}, bf16[2,4,32,256]{3,2,1,0:T(8,128)(2,1)S(1)}, u32[]{:S(2)}, u32[]{:S(2)}) collective-permute-start(bf16[2,4,32,256]{3,2,1,0:T(8,128)(2,1)S(1)} %get-tuple-element.186), channel_id=1, source_target_pairs={{0,32},{16,48},{32,0},{48,16},{64,96},{80,112},{96,64},{112,80},{1... | collective-permute-start | bytes 393224 | tf_op jit(solution)/shard_map/ppermute | solution.py:21
  372.4 9.1 %collective-permute-start.120 = (bf16[2,4,32,256]{3,2,1,0:T(8,128)(2,1)S(1)}, bf16[2,4,32,256]{3,2,1,0:T(8,128)(2,1)S(1)}, u32[]{:S(2)}, u32[]{:S(2)}) collective-permute-start(bf16[2,4,32,256]{3,2,1,0:T(8,128)(2,1)S(1)} %get-tuple-element.187), channel_id=1, source_target_pairs={{0,48},{16,32},{32,16},{48,0},{64,112},{80,96},{96,80},{112,64},{1... | collective-permute-start | bytes 393224 | tf_op jit(solution)/shard_map/ppermute | solution.py:21
  382.2 8.1 %collective-permute-start.115 = (bf16[2,4,32,256]{3,2,1,0:T(8,128)(2,1)S(1)}, bf16[2,4,32,256]{3,2,1,0:T(8,128)(2,1)S(1)}, u32[]{:S(2)}, u32[]{:S(2)}) collective-permute-start(bf16[2,4,32,256]{3,2,1,0:T(8,128)(2,1)S(1)} %get-tuple-element.182), channel_id=1, source_target_pairs={{0,8},{1,9},{2,10},{3,11},{4,12},{5,13},{6,14},{7,15},{8,0},{9,1},... | collective-permute-start | bytes 393224 | tf_op jit(solution)/shard_map/ppermute | solution.py:21
  384.3 8.0 %collective-permute-start.116 = (bf16[2,4,32,256]{3,2,1,0:T(8,128)(2,1)S(1)}, bf16[2,4,32,256]{3,2,1,0:T(8,128)(2,1)S(1)}, u32[]{:S(2)}, u32[]{:S(2)}) collective-permute-start(bf16[2,4,32,256]{3,2,1,0:T(8,128)(2,1)S(1)} %get-tuple-element.183), channel_id=1, source_target_pairs={{0,12},{1,13},{2,14},{3,15},{4,8},{5,9},{6,10},{7,11},{8,4},{9,5},... | collective-permute-start | bytes 393224 | tf_op jit(solution)/shard_map/ppermute | solution.py:21
  (106 other events, 582.6 us)
